TPU v7x, 128 devices: a whole 4x4x4 slice. The times are simulated.
128 devices in a mesh: dp: 8 (over x, y_lo), shard: 16 (over y_hi, z, core).
Axes of the slice: x: 4, y: 4 (y_hi: 2, y_lo: 2; y = y_hi * 2 + y_lo), z: 4, core: 2. Of those that a mesh axis runs over, the one named last changes fastest.
Arguments:
- tokens: bfloat16 [2, 16, 1024, 1024], P(None, 'shard', 'dp'), may hold values from -6 to 6
- cotangent: bfloat16 [2, 16, 1024, 1024], P(None, 'shard', 'dp'), may hold values from -6 to 6
- seq_lengths: int32 [2, 16, 16], P(None, 'shard'), may hold values from 16 to 192, as said below
- block_offsets: int32 [2, 16, 16], P(None, 'shard'), may hold values from 0 to 240, as said below
- deal_order: int32 [2, 16, 16], P(None, 'shard'), may hold values from 0 to 15, as said below
- w_query: bfloat16 [1024, 1024], P(('dp', 'shard')), may hold values from -0.25 to 0.25
- w_key: bfloat16 [1024, 1024], P(('dp', 'shard')), may hold values from -0.25 to 0.25
- w_value: bfloat16 [1024, 1024], P(('dp', 'shard')), may hold values from -0.1875 to 0.1875
- w_output: bfloat16 [1024, 1024], P(('dp', 'shard')), may hold values from -0.5 to 0.5
- b_query: bfloat16 [1024], P(('dp', 'shard')), may hold values from -3 to 3
- b_value: bfloat16 [1024], P(('dp', 'shard')), may hold values from -3 to 3
- b_output: bfloat16 [1024], P(('dp', 'shard')), may hold values from -3 to 3
- gain_one: bfloat16 [1024], P(('dp', 'shard')), may hold values from 0.25 to 1.75
- shift_one: bfloat16 [1024], P(('dp', 'shard')), may hold values from -3 to 3
- w_inner: bfloat16 [1024, 4096], P(('dp', 'shard')), may hold values from -0.1875 to 0.1875
- b_inner: bfloat16 [4096], P(('dp', 'shard')), may hold values from -3 to 3
- w_outer: bfloat16 [4096, 1024], P(('dp', 'shard')), may hold values from -0.09375 to 0.09375
- b_outer: bfloat16 [1024], P(('dp', 'shard')), may hold values from -3 to 3
- gain_two: bfloat16 [1024], P(('dp', 'shard')), may hold values from 0.25 to 1.75
- shift_two: bfloat16 [1024], P(('dp', 'shard')), may hold values from -3 to 3
Outputs:
- output: bfloat16 [2, 16, 1024, 1024], P(None, 'shard', 'dp')
- token_grad: bfloat16 [2, 16, 1024, 1024], P(None, 'shard', 'dp')
- grad_w_query: float32 [1024, 1024], P(('dp', 'shard'))
- grad_w_key: float32 [1024, 1024], P(('dp', 'shard'))
- grad_w_value: float32 [1024, 1024], P(('dp', 'shard'))
- grad_w_output: float32 [1024, 1024], P(('dp', 'shard'))
- grad_b_query: float32 [1024], P(('dp', 'shard'))
- grad_b_value: float32 [1024], P(('dp', 'shard'))
- grad_b_output: float32 [1024], P(('dp', 'shard'))
- grad_gain_one: float32 [1024], P(('dp', 'shard'))
- grad_shift_one: float32 [1024], P(('dp', 'shard'))
- grad_w_inner: float32 [1024, 4096], P(('dp', 'shard'))
- grad_b_inner: float32 [4096], P(('dp', 'shard'))
- grad_w_outer: float32 [4096, 1024], P(('dp', 'shard'))
- grad_b_outer: float32 [1024], P(('dp', 'shard'))
- grad_gain_two: float32 [1024], P(('dp', 'shard'))
- grad_shift_two: float32 [1024], P(('dp', 'shard'))
Inputs may be any that keep to these rules, and one draw needn't show every extreme that they name: `seq_lengths`: the sequences 2 d and 2 d + 1 of a group belong to block d; their lengths sum to at most 256, all lengths of a group sum to 1024, and in every group one block holds exactly 256 tokens. block_offsets[2 d + 1] = block_offsets[2 d] + seq_lengths[2 d] and block_offsets[2 d + 1] + seq_lengths[2 d + 1] <= 256. Each group's deal_order is a permutation of its sequences.
All inputs are finite; a program needn't handle non-finite values.
Results may differ from a plain program's by a relative error of at most 0.015.
Values may be sent and summed in bfloat16 or wider, within the bound.
A program may use at most 320 MiB of HBM per device.

v0:
```python
from functools import partial
import math

import jax
import jax.numpy as jnp
from jax import lax
from jax.sharding import PartitionSpec as P

D = 1024
HEADS = 16


norm_eps = 1e-05
masked_fill = -1e30


def side_by_side(arrays, axis, dim, along):
    columns = [a.reshape(*a.shape[:along], -1) for a in arrays]
    both = jnp.concatenate(columns, axis=along)
    whole, at, finished = (lax.all_gather(both, axis, axis=dim, tiled=True), 0, [])
    for a, column in zip(arrays, columns):
        share = whole[..., at : at + column.shape[along]]
        finished.append(share.reshape(*share.shape[:along], *a.shape[along:]))
        at += column.shape[along]
    return tuple(finished)


def sent_together(arrays, axis, dim, along):
    widths = [a.shape[along] for a in arrays]
    both = jnp.concatenate(arrays, axis=along)
    whole = lax.all_gather(both, axis, axis=dim, tiled=True)
    return tuple(jnp.split(whole, [sum(widths[:k]) for k in range(1, len(widths))], axis=along))


def split_up(shard, dim, peers):
    lengths = shard.shape
    parts = shard.reshape(*lengths[:dim], peers, lengths[dim] // peers, *lengths[dim + 1 :])
    return jnp.moveaxis(parts, dim, 0)


def sum_packed(arrays, axis, dims):
    peers = lax.axis_size(axis)
    parts = [split_up(a, dim, peers) for a, dim in zip(arrays, dims)]
    lines = jnp.concatenate([b.reshape(peers, -1) for b in parts], axis=1)
    rows = max(16, -(-lines.shape[1] // 1024) * 8)
    lines = jnp.pad(lines, ((0, 0), (0, rows * 128 - lines.shape[1]))).reshape(-1, 128)
    flat, at, finished = (lax.psum_scatter(lines, axis, tiled=True).reshape(-1), 0, [])
    for b in parts:
        part = b[0]
        finished.append(flat[at : at + part.size].reshape(part.shape))
        at += part.size
    return tuple(finished)


def matmul(left, right):
    return jnp.dot(left, right, preferred_element_type=jnp.float32)


def layer_norm(row_block, gain, shift):
    row_mean = jnp.mean(row_block, axis=-1, keepdims=True)
    centred = row_block - row_mean
    variance = jnp.mean(centred * centred, axis=-1, keepdims=True)
    return centred * lax.rsqrt(variance + norm_eps) * gain + shift


def route_tables(group_lengths, group_order):
    seq_count = group_order.shape[0]
    ordered = jnp.take(group_lengths, group_order)
    starts = jnp.cumsum(ordered) - ordered
    picked = group_order[:, None] == jnp.arange(seq_count)[None, :]
    anchor = jnp.sum(jnp.where(picked, starts[:, None], 0), axis=0)
    return (ordered, starts, anchor)


def device_rows(group_lengths, group_offsets, anchor, device, block_rows):
    positions = jnp.arange(block_rows)
    pair_ids = 2 * device + jnp.arange(2)
    first_row = jnp.take(group_offsets, pair_ids)
    counts = jnp.take(group_lengths, pair_ids)
    source_begin = jnp.take(anchor, pair_ids)
    inside = (positions[None, :] >= first_row[:, None]) & (
        positions[None, :] < (first_row + counts)[:, None]
    )
    segment = jnp.max(jnp.where(inside, pair_ids[:, None], -1), axis=0)
    source = jnp.sum(
        jnp.where(inside, source_begin[:, None] + positions[None, :] - first_row[:, None], 0),
        axis=0,
    )
    return (segment, source, jnp.any(inside, axis=0))


def return_index(ordered, starts, group_offsets, group_order, positions, block_rows):
    inside = (positions[:, None] >= starts[None, :]) & (
        positions[:, None] < (starts + ordered)[None, :]
    )
    target = group_order // 2 * block_rows + jnp.take(group_offsets, group_order)
    target = target[None, :] + positions[:, None] - starts[None, :]
    return jnp.sum(jnp.where(inside, target, 0), axis=1)


def head_scores(queries, key_rows, segment, score_scale):
    raw_scores = jnp.einsum("qhd,khd->hqk", queries, key_rows, preferred_element_type=jnp.float32)
    same_seq = (segment[:, None] == segment[None, :])[None]
    return (jnp.where(same_seq, raw_scores * score_scale, masked_fill), same_seq)


def encode_forward(row_block, segment, full):
    (
        w_query,
        w_key,
        w_value,
        w_output,
        b_query,
        b_value,
        b_output,
        gain_one,
        shift_one,
        w_inner,
        b_inner,
        w_outer,
        b_outer,
        gain_two,
        shift_two,
    ) = full
    row_count = row_block.shape[0]
    head_dim = D // HEADS
    score_scale = 1.0 / math.sqrt(head_dim)
    queries = (
        (matmul(row_block, w_query) + b_query)
        .astype(jnp.bfloat16)
        .reshape(row_count, HEADS, head_dim)
    )
    key_rows = matmul(row_block, w_key).astype(jnp.bfloat16).reshape(row_count, HEADS, head_dim)
    value_rows = (
        (matmul(row_block, w_value) + b_value)
        .astype(jnp.bfloat16)
        .reshape(row_count, HEADS, head_dim)
    )
    scores, same_seq = head_scores(queries, key_rows, segment, score_scale)
    highest = jnp.max(scores, axis=-1, keepdims=True)
    exp_terms = jnp.exp(scores - highest)
    exp_totals = jnp.sum(exp_terms, axis=-1, keepdims=True)
    attn_probs = (exp_terms / exp_totals).astype(jnp.bfloat16)
    log_total = highest + jnp.log(exp_totals)
    mixed_heads = jnp.einsum(
        "hqk,khd->qhd", attn_probs, value_rows, preferred_element_type=jnp.float32
    )
    context = mixed_heads.reshape(row_count, D).astype(jnp.bfloat16)
    attended = row_block.astype(jnp.float32) + (matmul(context, w_output) + b_output)
    normed = layer_norm(attended, gain_one.astype(jnp.float32), shift_one.astype(jnp.float32))
    normed_low = normed.astype(jnp.bfloat16)
    inner_pre = matmul(normed_low, w_inner) + b_inner
    activated = jax.nn.gelu(inner_pre, approximate=False).astype(jnp.bfloat16)
    outer_out = matmul(activated, w_outer) + b_outer
    final_sum = normed + outer_out
    encoded = layer_norm(final_sum, gain_two.astype(jnp.float32), shift_two.astype(jnp.float32))
    kept = (
        queries,
        key_rows,
        value_rows,
        log_total,
        context,
        attended,
        normed_low,
        inner_pre,
        activated,
        final_sum,
    )
    return (encoded, kept)


def encode_backward(row_block, segment, kept, full, cot_block):
    (
        w_query,
        w_key,
        w_value,
        w_output,
        b_query,
        b_value,
        b_output,
        gain_one,
        shift_one,
        w_inner,
        b_inner,
        w_outer,
        b_outer,
        gain_two,
        shift_two,
    ) = full
    (
        queries,
        key_rows,
        value_rows,
        log_total,
        context,
        attended,
        normed_low,
        inner_pre,
        activated,
        final_sum,
    ) = kept
    row_count = row_block.shape[0]
    head_dim = D // HEADS
    score_scale = 1.0 / math.sqrt(head_dim)
    ignored, pull_two = jax.vjp(
        layer_norm, final_sum, gain_two.astype(jnp.float32), shift_two.astype(jnp.float32)
    )
    d_final, grad_gain_two, grad_shift_two = pull_two(cot_block.astype(jnp.float32))
    d_outer = d_final.astype(jnp.bfloat16)
    grad_w_outer = jnp.einsum("rf,rd->fd", activated, d_outer, preferred_element_type=jnp.float32)
    grad_b_outer = jnp.sum(d_outer.astype(jnp.float32), axis=0)
    d_activated = jnp.einsum("rd,fd->rf", d_outer, w_outer, preferred_element_type=jnp.float32)
    ignored, pull_gelu = jax.vjp(partial(jax.nn.gelu, approximate=False), inner_pre)
    d_inner = pull_gelu(d_activated)[0].astype(jnp.bfloat16)
    grad_w_inner = jnp.einsum("rd,rf->df", normed_low, d_inner, preferred_element_type=jnp.float32)
    grad_b_inner = jnp.sum(d_inner.astype(jnp.float32), axis=0)
    d_normed = d_final + jnp.einsum(
        "rf,df->rd", d_inner, w_inner, preferred_element_type=jnp.float32
    )
    ignored, pull_one = jax.vjp(
        layer_norm, attended, gain_one.astype(jnp.float32), shift_one.astype(jnp.float32)
    )
    d_attended, grad_gain_one, grad_shift_one = pull_one(d_normed)
    d_branch = d_attended.astype(jnp.bfloat16)
    grad_w_output = jnp.einsum("rc,rd->cd", context, d_branch, preferred_element_type=jnp.float32)
    grad_b_output = jnp.sum(d_branch.astype(jnp.float32), axis=0)
    d_context = jnp.einsum("rd,cd->rc", d_branch, w_output, preferred_element_type=jnp.float32)
    d_context = d_context.astype(jnp.bfloat16).reshape(row_count, HEADS, head_dim)
    scores, same_seq = head_scores(queries, key_rows, segment, score_scale)
    probs_again = jnp.exp(scores - log_total)
    d_value = jnp.einsum(
        "hqk,qhd->khd",
        probs_again.astype(jnp.bfloat16),
        d_context,
        preferred_element_type=jnp.float32,
    )
    d_value = d_value.reshape(row_count, D).astype(jnp.bfloat16)
    d_probs = jnp.einsum("qhd,khd->hqk", d_context, value_rows, preferred_element_type=jnp.float32)
    d_scores = probs_again * (d_probs - jnp.sum(d_probs * probs_again, axis=-1, keepdims=True))
    d_raw = (jnp.where(same_seq, d_scores, 0.0) * score_scale).astype(jnp.bfloat16)
    d_query = jnp.einsum("hqk,khd->qhd", d_raw, key_rows, preferred_element_type=jnp.float32)
    d_query = d_query.reshape(row_count, D).astype(jnp.bfloat16)
    d_key = jnp.einsum("hqk,qhd->khd", d_raw, queries, preferred_element_type=jnp.float32)
    d_key = d_key.reshape(row_count, D).astype(jnp.bfloat16)
    grad_w_query = jnp.einsum("rd,rc->dc", row_block, d_query, preferred_element_type=jnp.float32)
    grad_b_query = jnp.sum(d_query.astype(jnp.float32), axis=0)
    grad_w_key = jnp.einsum("rd,rc->dc", row_block, d_key, preferred_element_type=jnp.float32)
    grad_w_value = jnp.einsum("rd,rc->dc", row_block, d_value, preferred_element_type=jnp.float32)
    grad_b_value = jnp.sum(d_value.astype(jnp.float32), axis=0)
    d_tokens = d_attended + jnp.einsum(
        "rc,dc->rd", d_query, w_query, preferred_element_type=jnp.float32
    )
    d_tokens = d_tokens + jnp.einsum("rc,dc->rd", d_key, w_key, preferred_element_type=jnp.float32)
    d_tokens = d_tokens + jnp.einsum(
        "rc,dc->rd", d_value, w_value, preferred_element_type=jnp.float32
    )
    block_grads = (
        grad_w_query,
        grad_w_key,
        grad_w_value,
        grad_w_output,
        grad_b_query,
        grad_b_value,
        grad_b_output,
        grad_gain_one,
        grad_shift_one,
        grad_w_inner,
        grad_b_inner,
        grad_w_outer,
        grad_b_outer,
        grad_gain_two,
        grad_shift_two,
    )
    return (d_tokens.astype(jnp.bfloat16), block_grads)


def local(
    tokens,
    cotangent,
    seq_lengths,
    block_offsets,
    deal_order,
    w_query,
    w_key,
    w_value,
    w_output,
    b_query,
    b_value,
    b_output,
    gain_one,
    shift_one,
    w_inner,
    b_inner,
    w_outer,
    b_outer,
    gain_two,
    shift_two,
):
    micro_count = tokens.shape[0]
    tok_local = tokens.shape[2]
    width = tokens.shape[3]
    block_rows = 2 * tok_local
    device = lax.axis_index("dp")
    shard_count = lax.axis_size(("dp", "shard"))
    shards_in = (
        w_query,
        w_key,
        w_value,
        w_output,
        b_query,
        b_value,
        b_output,
        gain_one,
        shift_one,
        w_inner,
        b_inner,
        w_outer,
        b_outer,
        gain_two,
        shift_two,
    )
    running = tuple(
        (
            jnp.zeros((shard_part.shape[0] * shard_count,) + shard_part.shape[1:], jnp.float32)
            for shard_part in shards_in
        )
    )
    outputs = []
    token_grads = []
    for micro_step in range(micro_count):
        full = (
            *side_by_side(
                (
                    w_query,
                    w_key,
                    w_value,
                    w_output,
                    b_query,
                    b_value,
                    b_output,
                    gain_one,
                    shift_one,
                    w_inner,
                ),
                ("dp", "shard"),
                0,
                1,
            ),
            *side_by_side((b_inner, w_outer), ("dp", "shard"), 0, 1),
            lax.all_gather(b_outer, ("dp", "shard"), axis=0, tiled=True),
            lax.all_gather(gain_two, ("dp", "shard"), axis=0, tiled=True),
            lax.all_gather(shift_two, ("dp", "shard"), axis=0, tiled=True),
        )
        group_lengths = seq_lengths[micro_step, 0]
        group_offsets = block_offsets[micro_step, 0]
        group_order = deal_order[micro_step, 0]
        ordered, starts, anchor = route_tables(group_lengths, group_order)
        segment, source, valid = device_rows(
            group_lengths, group_offsets, anchor, device, block_rows
        )
        empty_block = jnp.zeros((block_rows, width), jnp.bfloat16)
        pieces = sent_together((tokens[micro_step, 0], cotangent[micro_step, 0]), "dp", 0, 1)
        piece_rows = pieces[0].shape[0]
        inside = valid & (source >= 0) & (source < piece_rows)
        row_index = jnp.clip(source, 0, piece_rows - 1)
        dealt_rows = jnp.where(inside[:, None], jnp.take(pieces[0], row_index, axis=0), empty_block)
        dealt_cot = jnp.where(inside[:, None], jnp.take(pieces[1], row_index, axis=0), empty_block)
        encoded, kept = encode_forward(dealt_rows, segment, full)
        d_tokens, block_grads = encode_backward(dealt_rows, segment, kept, full, dealt_cot)
        running = tuple((current + addend for current, addend in zip(running, block_grads)))
        positions = device * tok_local + jnp.arange(tok_local)
        target = return_index(ordered, starts, group_offsets, group_order, positions, block_rows)
        empty_rows = jnp.zeros((tok_local, width), jnp.bfloat16)
        place_pieces = sent_together((encoded.astype(jnp.bfloat16), d_tokens), "dp", 0, 1)
        place_piece_rows = place_pieces[0].shape[0]
        place_inside = (target >= 0) & (target < place_piece_rows)
        place_row_index = jnp.clip(target, 0, place_piece_rows - 1)
        out_rows = jnp.where(
            place_inside[:, None], jnp.take(place_pieces[0], place_row_index, axis=0), empty_rows
        )
        grad_rows = jnp.where(
            place_inside[:, None], jnp.take(place_pieces[1], place_row_index, axis=0), empty_rows
        )
        outputs.append(out_rows)
        token_grads.append(grad_rows)
    owned = sum_packed(
        (
            running[0],
            running[1],
            running[2],
            running[3],
            running[4],
            running[5],
            running[6],
            running[7],
            running[8],
            running[9],
            running[10],
            running[11],
            running[12],
            running[13],
            running[14],
        ),
        ("dp", "shard"),
        (0, 0, 0, 0, 0, 0, 0, 0, 0, 0, 0, 0, 0, 0, 0),
    )
    return (
        jnp.stack(outputs)[:, None],
        jnp.stack(token_grads)[:, None],
        owned[0],
        owned[1],
        owned[2],
        owned[3],
        owned[4],
        owned[5],
        owned[6],
        owned[7],
        owned[8],
        owned[9],
        owned[10],
        owned[11],
        owned[12],
        owned[13],
        owned[14],
    )


def solution(mesh):
    in_specs = (
        P(None, "shard", "dp", None),
        P(None, "shard", "dp", None),
        P(None, "shard", None),
        P(None, "shard", None),
        P(None, "shard", None),
        P(("dp", "shard"), None),
        P(("dp", "shard"), None),
        P(("dp", "shard"), None),
        P(("dp", "shard"), None),
        P(("dp", "shard")),
        P(("dp", "shard")),
        P(("dp", "shard")),
        P(("dp", "shard")),
        P(("dp", "shard")),
        P(("dp", "shard"), None),
        P(("dp", "shard")),
        P(("dp", "shard"), None),
        P(("dp", "shard")),
        P(("dp", "shard")),
        P(("dp", "shard")),
    )
    out_specs = (
        P(None, "shard", "dp", None),
        P(None, "shard", "dp", None),
        P(("dp", "shard"), None),
        P(("dp", "shard"), None),
        P(("dp", "shard"), None),
        P(("dp", "shard"), None),
        P(("dp", "shard")),
        P(("dp", "shard")),
        P(("dp", "shard")),
        P(("dp", "shard")),
        P(("dp", "shard")),
        P(("dp", "shard"), None),
        P(("dp", "shard")),
        P(("dp", "shard"), None),
        P(("dp", "shard")),
        P(("dp", "shard")),
        P(("dp", "shard")),
    )
    return jax.shard_map(local, mesh=mesh, in_specs=in_specs, out_specs=out_specs, check_vma=False)
```

profile of v0, /device:TPU:1, one launch (start us, length us, event | category | flops | bytes accessed | tf_op | source)
XLA Modules:
  0.0 1525.7 jit_solution(13528722368655933085)
XLA Ops:
  21.4 83.8 %all-reduce.5 = (bf16[1024]{0:T(1024)(128)(2,1)S(1)}, bf16[1024]{0:T(1024)(128)(2,1)S(1)}, bf16[1024]{0:T(1024)(128)(2,1)S(1)}) all-reduce(bf16[1024]{0:T(1024)(128)(2,1)S(1)} %dynamic-update-slice, bf16[1024]{0:T(1024)(128)(2,1)S(1)} %dynamic-update-slice.1, ...), channel_id=1, replica_groups=mesh['dp'=8,'shard'=16] {'dp','shard'}, use_global_device_ids=true, to_apply=%add.1 | all-reduce | flops 3072 | bytes 12288
  117.7 80.1 %all-gather.15.cloned.1.call-done = bf16[1024,2048]{1,0:T(8,128)(2,1)} async-done(((bf16[128,2048]{1,0:T(8,128)(2,1)}), bf16[1024,2048]{1,0:T(8,128)(2,1)}) %all-gather.15.cloned.1.call-update) | async-done | bytes 4194320 | tf_op jit(solution)/shard_map/all_gather | solution.py:31
  207.2 200.9 %all-gather.11.cloned.1.call-done = bf16[4096,1025]{1,0:T(8,128)(2,1)} async-done(((bf16[32,1025]{1,0:T(8,128)(2,1)}), bf16[4096,1025]{1,0:T(8,128)(2,1)}) %all-gather.11.cloned.1.call-update) | async-done | bytes 8396816 | tf_op jit(solution)/shard_map/all_gather | solution.py:20
  410.3 213.2 %all-gather.9.cloned.1.call-done = bf16[1024,8197]{1,0:T(8,128)(2,1)} async-done(((bf16[8,8197]{1,0:T(8,128)(2,1)}), bf16[1024,8197]{1,0:T(8,128)(2,1)}) %all-gather.9.cloned.1.call-update) | async-done | bytes 16787472 | tf_op jit(solution)/shard_map/all_gather | solution.py:20
  661.2 14.7 multiply_convert_fusion.3
  680.3 14.5 multiply_convert_fusion.1
  694.8 8.2 fusion.228
  709.5 10.8 convert_reduce_fusion
  720.3 7.5 fusion.106
  727.8 10.8 convert_reduce_fusion.1
  738.6 7.4 multiply_reduce_fusion.3
  757.9 8.9 convert_reduce_fusion.11
  766.9 8.9 fusion.162
  798.3 9.0 convert_reduce_fusion.12
  807.3 9.0 fusion.168
  873.7 9.9 convolution_add_fusion.1
  883.6 18.4 %reshape_reshape.22 = f32[128,32768]{1,0:T(8,128)} reshape(f32[1024,4096]{1,0:T(8,128)} %convolution_add_fusion.1) | data formatting | bytes 33554432 | tf_op jit(solution)/shard_map/reshape;reshape | solution.py:44
  906.9 9.2 convolution_add_fusion
  916.2 18.3 %reshape_reshape.23 = f32[128,32768]{1,0:T(8,128)} reshape(f32[4096,1024]{1,0:T(8,128)} %convolution_add_fusion) | data formatting | bytes 33554432 | tf_op jit(solution)/shard_map/reshape;reshape | solution.py:44
  957.9 56.1 %dynamic-update-slice.12 = f32[128,98400]{1,0:T(8,128)} dynamic-update-slice(f32[128,98400]{1,0:T(8,128)} %dynamic-update-slice.11, f32[128,32768]{1,0:T(8,128)} %reshape_reshape.22, s32[]{} %constant.232, s32[]{} %constant.241) | dynamic-update-slice | bytes 33554436
  1015.6 54.8 %dynamic-update-slice.14 = f32[128,98400]{1,0:T(8,128)} dynamic-update-slice(f32[128,98400]{1,0:T(8,128)} %dynamic-update-slice.13, f32[128,32768]{1,0:T(8,128)} %reshape_reshape.23, s32[]{} %constant.232, s32[]{} %constant.243) | dynamic-update-slice | bytes 33554436
  1075.2 33.9 %pad.4 = f32[128,99328]{1,0:T(8,128)} pad(f32[128,98400]{1,0:T(8,128)} %dynamic-update-slice.17, f32[]{:T(128)} %constant.101.clone.1), padding=0_0x0_928 | pad | bytes 101236736 | tf_op jit(solution)/shard_map/jit(_pad)/pad | solution.py:46
  1109.1 38.1 %reshape.559 = f32[99328,128]{1,0:T(8,128)} reshape(f32[128,99328]{1,0:T(8,128)} %pad.4) | data formatting | bytes 101711872 | tf_op jit(solution)/shard_map/reshape | solution.py:46
  1178.9 332.5 %all-reduce.8.cloned.1.call-done = f32[99328,128]{1,0:T(8,128)} async-done(((f32[99328,128]{1,0:T(8,128)}), f32[99328,128]{1,0:T(8,128)}) %all-reduce.8.cloned.1.call-update) | async-done | bytes 50855952
  (499 shorter events, 250.3 us)
Async XLA Ops:
  7.3 101.0 %all-gather.7.cloned.1.call-start = ((), (), s32[]{:S(2)}) async-start(), calls=%async_computation | async-start | bytes 4718592 | tf_op jit(solution)/shard_map/all_gather | solution.py:31
  9.6 188.2 %all-gather.15.cloned.1.call-start = ((), (), s32[]{:S(2)}) async-start(), calls=%async_computation.4 | async-start | bytes 4718592 | tf_op jit(solution)/shard_map/all_gather | solution.py:31
  10.5 397.6 %all-gather.11.cloned.1.call-start = ((), (), s32[]{:S(2)}) async-start(), calls=%async_computation.2 | async-start | bytes 9510912 | tf_op jit(solution)/shard_map/all_gather | solution.py:20
  11.4 612.1 %all-gather.9.cloned.1.call-start = ((), (), s32[]{:S(2)}) async-start(), calls=%async_computation.1 | async-start | bytes 17172480 | tf_op jit(solution)/shard_map/all_gather | solution.py:20
  12.8 1135.3 %all-gather.17.cloned.1.call-start = ((), (), s32[]{:S(2)}) async-start(), calls=%async_computation.5 | async-start | bytes 9437184 | tf_op jit(solution)/shard_map/all_gather | solution.py:31
  18.9 89.4 %copy-start.98 = (s32[16]{0:T(128)}, s32[16]{0:T(128)S(1)}, u32[]{:S(2)}) copy-start(s32[16]{0:T(128)S(1)} %reduce.15) | copy-start | bytes 196
  107.4 516.1 %copy-start.67 = (pred[256]{0:T(512)(128)(4,1)}, pred[256]{0:T(512)(128)(4,1)S(1)}, u32[]{:S(2)}) copy-start(pred[256]{0:T(512)(128)(4,1)S(1)} %get-tuple-element.190) | copy-start | bytes 772
  107.4 516.1 %copy-start.70 = (pred[256]{0:T(512)(128)(4,1)}, pred[256]{0:T(512)(128)(4,1)S(1)}, u32[]{:S(2)}) copy-start(pred[256]{0:T(512)(128)(4,1)S(1)} %get-tuple-element.191) | copy-start | bytes 772
  107.5 528.3 %copy-start.73 = (pred[256]{0:T(512)(128)(4,1)}, pred[256]{0:T(512)(128)(4,1)S(1)}, u32[]{:S(2)}) copy-start(pred[256]{0:T(512)(128)(4,1)S(1)} %get-tuple-element.184) | copy-start | bytes 772
  107.5 528.3 %copy-start.76 = (pred[256]{0:T(512)(128)(4,1)}, pred[256]{0:T(512)(128)(4,1)S(1)}, u32[]{:S(2)}) copy-start(pred[256]{0:T(512)(128)(4,1)S(1)} %get-tuple-element.185) | copy-start | bytes 772
  107.6 531.0 %copy-start.51 = (pred[256,256]{0,1:T(8,128)(4,1)}, pred[256,256]{0,1:T(8,128)(4,1)S(1)}, u32[]{:S(2)}) copy-start(pred[256,256]{0,1:T(8,128)(4,1)S(1)} %broadcast_compare_fusion.1) | copy-start | bytes 196612
  115.7 520.0 %copy-start.8 = (bf16[256,1024]{1,0:T(8,128)(2,1)}, bf16[256,1024]{1,0:T(8,128)(2,1)S(1)}, u32[]{:S(2)}) copy-start(bf16[256,1024]{1,0:T(8,128)(2,1)S(1)} %gather_fusion.5) | copy-start | bytes 1572868
  657.0 18.9 %slice-start.5 = ((s8[9437184]{0:T(1024)(128)(4,1)}), s8[4194304]{0:T(1024)(128)(4,1)S(1)}, s32[]{:S(2)}) async-start(s8[9437184]{0:T(1024)(128)(4,1)} %bitcast.182), calls=%async_computation.12 | async-start | bytes 8388608
  660.3 85.8 %copy-start.63 = (f32[256]{0:T(256)}, f32[256]{0:T(256)S(1)}, u32[]{:S(2)}) copy-start(f32[256]{0:T(256)S(1)} %broadcast_multiply_fusion.1) | copy-start | bytes 3076
  660.5 85.5 %copy-start.94 = (f32[256]{0:T(256)}, f32[256]{0:T(256)S(1)}, u32[]{:S(2)}) copy-start(f32[256]{0:T(256)S(1)} %fusion.187) | copy-start | bytes 3076
  787.5 375.1 %all-gather.13.cloned.1.call-start = ((), (), s32[]{:S(2)}) async-start(), calls=%async_computation.3 | async-start | bytes 9437184 | tf_op jit(solution)/shard_map/all_gather | solution.py:31
  826.9 684.6 %all-reduce.8.cloned.1.call-start = ((), (), s32[]{:S(2)}) async-start(), calls=%async_computation.6 | async-start | bytes 101711872
  883.6 18.4 %copy-start.90 = (f32[4096]{0:T(1024)S(1)}, f32[4096]{0:T(1024)}, u32[]{:S(2)}) copy-start(f32[4096]{0:T(1024)} %get-tuple-element.233) | copy-start | bytes 49156
  883.6 18.4 %copy-start.91 = (f32[4096]{0:T(1024)S(1)}, f32[4096]{0:T(1024)}, u32[]{:S(2)}) copy-start(f32[4096]{0:T(1024)} %get-tuple-element.231) | copy-start | bytes 49156
  883.6 19.2 %copy-start.26 = (bf16[256,1024]{1,0:T(8,128)(2,1)S(1)}, bf16[256,1024]{1,0:T(8,128)(2,1)}, u32[]{:S(2)}) copy-start(bf16[256,1024]{1,0:T(8,128)(2,1)} %copy-done.25) | copy-start | bytes 1572868
  916.2 18.4 %copy-start.83 = (f32[1024]{0:T(1024)S(1)}, f32[1024]{0:T(1024)}, u32[]{:S(2)}) copy-start(f32[1024]{0:T(1024)} %get-tuple-element.179) | copy-start | bytes 12292
  916.2 18.5 %copy-start.80 = (f32[1024]{0:T(1024)S(1)}, f32[1024]{0:T(1024)}, u32[]{:S(2)}) copy-start(f32[1024]{0:T(1024)} %get-tuple-element.105) | copy-start | bytes 12292
  916.2 18.5 %copy-start.81 = (f32[1024]{0:T(1024)S(1)}, f32[1024]{0:T(1024)}, u32[]{:S(2)}) copy-start(f32[1024]{0:T(1024)} %get-tuple-element.177) | copy-start | bytes 12292
  957.9 56.1 %copy-start.45 = (f32[128,32]{1,0:T(8,128)S(1)}, f32[128,32]{1,0:T(8,128)}, u32[]{:S(2)}) copy-start(f32[128,32]{1,0:T(8,128)} %add.452) | copy-start | bytes 49156
  (119 other events, 631.1 us)
Sparse Core Ops, SparseCore 0:
  10.4 94.4 all-gather.6
  107.1 90.6 all-gather.14
  200.1 207.9 all-gather.10
  409.7 213.7 all-gather.8
  787.6 167.0 all-gather.16
  956.2 173.6 all-gather.12
  1147.4 364.0 all-reduce.7
where the time goes:
time: 1540 us; the launch traced here: 1530 us
  waiting for transfers between devices  827 us (54%)
  local copies, waits for them, and re-layouts  352 us (23%)
  matrix products  218 us (14%)
  blocking collectives  83.8 us (5%)
  other arithmetic  28.2 us (2%)
  between operations  16.3 us (1%)
    all_gather x2, waiting for transfers between devices, side_by_side(): lax.all_gather(both, axis, axis=dim, tiled=True)  414 us
    unnamed x8, waiting for transfers between devices  333 us
    unnamed x292, local copies, waits for them, and re-layouts  148 us
    unnamed x1, blocking collectives  83.8 us
    all_gather x4, waiting for transfers between devices, sent_together(): whole = lax.all_gather(both, axis, axis=dim, tiled=True)  80.1 us
    dot_general x12, matrix products, matmul(): return jnp.dot(left, right, preferred_element_type=jnp.float32)  63.3 us
    another operation x6, local copies, waits for them, and re-layouts, sum_packed(): lines = jnp.concatenate([b.reshape(peers, -1) for b in parts], axis=1)  57.1 us
    reshape x1, local copies, waits for them, and re-layouts, sum_packed(): jnp.pad(lines, ((0, 0), (0, rows * 128 - lines.shape[1]))).reshape(-1, 128)  38.1 us
  transfers between devices with their start and end apart: 7, of which 4 were waited for; matrix products, arithmetic and copies ran while one was open for 28% of the time, Pallas kernels for 0%

commit v1 on v0

v1 whole, which is shorter than its diff:
```python
import math

import jax
import jax.numpy as jnp
from jax import lax
from jax.experimental import pallas as pl
from jax.experimental.pallas import tpu as pltpu
from jax.sharding import PartitionSpec as P

MESH = pl.DeviceIdType.MESH
BF = jnp.bfloat16
F32 = jnp.float32
D = 1024
FF = 4096
HEADS = 16
HEAD = 64
TOK = 128
OWN = 2 * TOK
HALO = 192
WIN = OWN + 2 * HALO
AXES = ("x", "y", "z")
ORDER = (("z", "y", "x"), ("x", "z", "y"), ("y", "x", "z"))
CHIPS = (4, 2, 2, 4)
N_SEM = 200


def position():
    dp, sh = lax.axis_index("dp"), lax.axis_index("shard")
    return {
        "x": lax.div(dp, 2),
        "y": lax.div(sh, 8) * 2 + lax.rem(dp, 2),
        "z": lax.div(lax.rem(sh, 8), 2),
        "c": lax.rem(sh, 2),
    }


def device_at(at):
    return (
        at["x"] * 2 + lax.rem(at["y"], 2),
        lax.div(at["y"], 2) * 8 + at["z"] * 2 + at["c"],
    )


class Net:
    def __init__(self, send_sem, recv_sem):
        self.me = position()
        self.send_sem, self.recv_sem = send_sem, recv_sem
        self.used = 0
        self.sent = []

    def moved(self, axis, by):
        at = dict(self.me)
        if axis == "c":
            at["c"] = 1 - at["c"]
        else:
            at[axis] = lax.rem(at[axis] + by, 4)
        return at

    def ring(self, axis, by):
        return device_at(self.moved(axis, by))

    def pair(self, by, lo):
        at = self.moved("x", by % 4)
        at["y"] = lax.div(at["y"], 2) * 2 + lo
        return device_at(at)

    def slot(self):
        self.used += 1
        return self.used - 1

    def make(self, src, dst, device, send, recv):
        return pltpu.make_async_remote_copy(
            src_ref=src,
            dst_ref=dst,
            send_sem=self.send_sem.at[send],
            recv_sem=self.recv_sem.at[recv],
            device_id=device,
            device_id_type=MESH,
        )

    def copy(self, src, dst, device):
        k = self.slot()
        moved = self.make(src, dst, device, k, k)
        moved.start()
        self.sent.append(moved)
        return moved

    def barrier(self):
        bar = pltpu.get_barrier_semaphore()
        peers = [self.ring("c", 0)] + [self.ring(a, b) for a in AXES for b in (1, 2, 3)]
        other = 1 - lax.rem(self.me["y"], 2)
        peers += [self.pair(1, other), self.pair(3, other)]
        for p in peers:
            pl.semaphore_signal(bar, inc=1, device_id=p, device_id_type=MESH)
        pl.semaphore_wait(bar, len(peers))

    def finish(self):
        for moved in self.sent:
            moved.wait_send()
        assert self.used <= N_SEM, self.used


def chip_index(at, drop=()):
    out = []
    for axis in AXES:
        if axis in drop:
            continue
        v = at[axis]
        if axis == "y":
            if v is None:
                out += [slice(None), slice(None)]
            elif isinstance(v, tuple):
                out += [v[1], slice(None)]
            else:
                out += [lax.rem(v, 2), lax.div(v, 2)]
        elif v is None:
            out.append(slice(None))
        elif isinstance(v, tuple):
            out.append(pl.ds(2 * v[1], 2))
        else:
            out.append(v)
    return tuple(out)


def chip_shape(drop):
    shape = ()
    for axis in AXES:
        if axis not in drop:
            shape += (2, 2) if axis == "y" else (4,)
    return shape


def columns(base, width):
    return pl.ds(pl.multiple_of(base, 128), width)


class Gather:
    def __init__(self, net, ref, rows, cols, order):
        self.net, self.ref, self.rows, self.cols = net, ref, rows, cols
        self.a, self.b, self.e = order

    def at(self, **over):
        place = {k: self.net.me[k] for k in AXES}
        place.update(over)
        return self.ref.at[chip_index(place) + (self.rows, self.cols)]

    def send(self, region, axis, by):
        return self.net.copy(region, region, self.net.ring(axis, by))

    def p1(self):
        self.c = [self.send(self.at(), self.a, d) for d in (1, 3, 2)]

    def p2(self):
        for moved in self.c:
            moved.wait_recv()
        self.c = [self.send(self.at(**{self.a: None}), self.b, d) for d in (1, 3, 2)]

    def part(self, h, by):
        e = self.net.moved(self.e, by)[self.e]
        return self.at(**{self.a: h if h is None else ("half", h), self.b: None, self.e: e})

    def p3(self):
        for moved in self.c:
            moved.wait_recv()
        self.r0 = self.send(self.part(0, 0), self.e, 1)
        self.l1 = self.send(self.part(1, 0), self.e, 3)
        self.r1 = self.send(self.part(1, 0), self.e, 1)
        self.l0 = self.send(self.part(0, 0), self.e, 3)
        self.core = [self.send(self.part(None, 0), "c", 0)]

    def p3_mid(self):
        self.r0.wait_recv()
        self.f0 = self.send(self.part(0, 3), self.e, 1)
        self.l1.wait_recv()
        self.f1 = self.send(self.part(1, 1), self.e, 3)

    def p3_core(self):
        self.r1.wait_recv()
        self.core.append(self.send(self.part(None, 3), "c", 0))
        self.l0.wait_recv()
        self.core.append(self.send(self.part(None, 1), "c", 0))

    def p3_end(self):
        self.f0.wait_recv()
        self.f1.wait_recv()
        self.core.append(self.send(self.part(None, 2), "c", 0))

    def done(self):
        for moved in self.core:
            moved.wait_recv()


def each(lanes, step):
    for lane in lanes:
        getattr(lane, step)()


def pieces(lo):
    at = TOK * lo
    return (
        (1, pl.ds(TOK // 2, TOK // 2), at + TOK // 2 - (OWN - HALO), None),
        (1, pl.ds(0, TOK // 2), at - (OWN - HALO), 1),
        (-1, pl.ds(0, TOK // 2), at + HALO + OWN, None),
        (-1, pl.ds(TOK // 2, TOK // 2), at + TOK // 2 + HALO + OWN, 0),
    )


def rows_at(base, count):
    return pl.ds(pl.multiple_of(base, TOK // 2), count)


class Window:
    def __init__(self, net, tokens, cotangent, window, cots, local_sem):
        self.net = net
        lo = lax.rem(net.me["y"], 2)
        other = 1 - lo
        self.copies = []
        mine = rows_at(HALO + TOK * lo, TOK)
        theirs = rows_at(TOK * lo, TOK)
        self.local = [
            pltpu.make_async_copy(tokens.at[lo], window.at[mine], local_sem.at[0]),
            pltpu.make_async_copy(cotangent.at[lo], cots.at[theirs], local_sem.at[1]),
        ]
        self.pair = [
            (tokens.at[other], window.at[mine]),
            (cotangent.at[other], cots.at[theirs]),
        ]
        self.halo = []
        for by, rows, to, only in pieces(lo):
            first = net.slot()
            second = net.slot()
            for m in range(2):
                send = first if m == 0 else second
                copy = net.make(
                    tokens.at[m, rows], window.at[rows_at(to, TOK // 2)], net.pair(by, m), send, first + lo
                )
                self.halo.append((copy, only))
        self.gets = []
        for k, (by, rows, to, only) in enumerate(pieces(lo)):
            for source in range(2):
                if only is None or only == source:
                    index = 2 * k + source + (net.used - 8)
                    self.gets.append(
                        net.make(tokens.at[0, rows], window.at[pl.ds(0, TOK // 2)], net.pair(1, other), 0, index)
                    )

    def start(self):
        for copy in self.local:
            copy.start()
        lo = lax.rem(self.net.me["y"], 2)
        self.pair = [self.net.copy(s, d, self.net.pair(0, 1 - lo)) for s, d in self.pair]
        for copy, only in self.halo:
            if only is None:
                copy.start()
            else:
                pl.when(lo == only)(copy.start)

    def done(self):
        for copy in self.local:
            copy.wait()
        for copy in self.pair + self.gets:
            copy.wait_recv()

    def finish(self):
        lo = lax.rem(self.net.me["y"], 2)
        for copy, only in self.halo:
            if only is None:
                copy.wait_send()
            else:
                pl.when(lo == only)(copy.wait_send)


def place_own(me, mine, peer, full):
    here = chip_index(me)
    c = me["c"]
    first = c == 0

    def both(a, b):
        return jnp.concatenate([jnp.where(first, a, b), jnp.where(first, b, a)], axis=0)

    half = columns(c * 512, 512)
    for j in range(4):
        r = slice(8 * j, 8 * j + 8)
        full[j][here + (slice(None), half)] = both(mine[r, half], peer[r, half])
    for t in range(2):
        r, s = slice(32 + 8 * t, 40 + 8 * t), slice(48 + 8 * t, 56 + 8 * t)
        a = jnp.where(first, mine[r, :], mine[s, :])
        b = jnp.where(first, peer[r, :], peer[s, :])
        full[4][here + (slice(None), columns(c * 2048 + 1024 * t, 1024))] = both(a, b)
    full[5][here + (slice(None), half)] = both(mine[64:96, half], peer[64:96, half])


def gather_kernel(own, tokens, cotangent, *refs):
    outs, rest = refs[:8], refs[8:]
    mine, peer = rest[:2]
    full = rest[2:8]
    send_sem, recv_sem, local_sem = rest[8:]
    net = Net(send_sem, recv_sem)
    c = net.me["c"]
    load = pltpu.make_async_copy(own, mine, local_sem.at[0])
    load.start()
    net.barrier()
    load.wait()
    swap = net.copy(mine, peer, net.ring("c", 0))
    window = Window(net, tokens, cotangent, outs[6], outs[7], local_sem)
    window.start()
    swap.wait_recv()
    place_own(net.me, mine, peer, full)
    rows = slice(None)
    half = columns(c * 512, 512)
    wi, wu = full[4], full[5]
    first = [Gather(net, full[j], rows, half, ORDER[j]) for j in range(3)]
    second = [
        Gather(net, full[3], rows, half, ORDER[0]),
        Gather(net, wi, rows, columns(c * 2048 + 512, 1024), ORDER[1]),
        Gather(net, wi, rows, columns(c * 2048 + 1536, 512), ORDER[2]),
        Gather(net, wi, rows, columns(c * 2048, 512), ORDER[0]),
    ]
    third = [
        Gather(net, wu, pl.ds(0, 16), half, ORDER[0]),
        Gather(net, wu, pl.ds(16, 16), half, ORDER[1]),
        Gather(net, wu, pl.ds(32, 32), half, ORDER[2]),
    ]
    for step in ("p1", "p2"):
        for lanes in (first, second, third):
            each(lanes, step)
    each(first, "p3")
    each(second, "p3")
    each(first, "p3_mid")
    each(first, "p3_core")
    each(third, "p3")
    each(first, "p3_end")
    each(first, "done")
    for step in ("p3_mid", "p3_core", "p3_end"):
        each(second, step)
    each(third, "p3_mid")
    each(third, "p3_core")
    each(second, "done")
    each(third, "p3_end")
    each(third, "done")
    window.done()
    stores = [pltpu.make_async_copy(w, o, local_sem.at[2 + k]) for k, (w, o) in enumerate(zip(full, outs))]
    for store in stores:
        store.start()
    for store in stores:
        store.wait()
    window.finish()
    net.finish()


BLOCKS = ((16, 1024),) * 4 + ((16, 4096), (64, 1024))


def gather_all(own, tokens, cotangent):
    any_space = pl.BlockSpec(memory_space=pl.ANY)
    full = [CHIPS + s for s in BLOCKS]
    return pl.pallas_call(
        gather_kernel,
        name="gather_all",
        out_shape=[jax.ShapeDtypeStruct(s, BF) for s in full + [(WIN, D), (OWN, D)]],
        in_specs=[any_space] * 3,
        out_specs=[any_space] * 8,
        scratch_shapes=[pltpu.VMEM((96, 1024), BF)] * 2
        + [pltpu.VMEM(s, BF) for s in full]
        + [
            pltpu.SemaphoreType.DMA((N_SEM,)),
            pltpu.SemaphoreType.DMA((N_SEM,)),
            pltpu.SemaphoreType.DMA((8,)),
        ],
        compiler_params=pltpu.CompilerParams(collective_id=1, has_side_effects=True, vmem_limit_bytes=50 << 20),
    )(own, tokens, cotangent)


def add_into(dst, srcs):
    lead = dst.shape[:-2]
    loop = lead[:-1] if len(lead) > 1 else lead
    total = math.prod(loop)

    def body(k, carry):
        index, rest = (), k
        for n in reversed(loop):
            index = (lax.rem(rest, n),) + index
            rest = lax.div(rest, n)
        value = dst[index].astype(F32)
        for s in srcs:
            value = value + s[index].astype(F32)
        dst[index] = value.astype(BF)
        return carry

    lax.fori_loop(0, total, body, 0)


class Reduce:
    def __init__(self, net, ref, rows, base, width, other_base, order, bufs):
        self.net, self.ref, self.rows, self.width = net, ref, rows, width
        self.mine, self.theirs = columns(base, width), columns(other_base, width)
        self.a, self.b, self.e = order
        self.sib, self.wide, self.mid, self.low = bufs

    def at(self, cols=None, **over):
        place = {k: self.net.me[k] for k in AXES}
        place.update(over)
        return self.ref.at[chip_index(place) + (self.rows, self.mine if cols is None else cols)]

    def near(self, by):
        return self.net.moved(self.a, by)[self.a]

    def quarter(self, by, h):
        b = None if h is None else ("half", h)
        return self.at(**{self.a: self.near(by), self.b: b, self.e: None})

    def buf(self, k, h):
        b = None if h is None else ("half", h)
        return self.wide.at[(k,) + chip_index({self.b: b, self.e: None}, drop=(self.a,))]

    def d0(self):
        every = {k: None for k in AXES}
        self.c = self.net.copy(self.at(cols=self.theirs, **every), self.sib, self.net.ring("c", 0))

    def send(self, by, h, k, to):
        return self.net.copy(self.quarter(by, h), self.buf(k, h), self.net.ring(self.a, to))

    def p1(self):
        self.c.wait_recv()
        add_into(self.at(**{k: None for k in AXES}), [self.sib])
        self.m0 = self.send(2, 0, 0, 1)
        self.m1 = self.send(2, 1, 0, 3)
        self.l1 = self.send(1, 1, 1, 1)
        self.r0 = self.send(3, 0, 2, 3)

    def p1_mid(self):
        self.m0.wait_recv()
        add_into(self.quarter(1, 0), [self.buf(0, 0)])
        self.l0 = self.send(1, 0, 1, 1)
        self.m1.wait_recv()
        add_into(self.quarter(3, 1), [self.buf(0, 1)])
        self.r1 = self.send(3, 1, 2, 3)

    def p2(self):
        for moved in (self.l1, self.r0, self.l0, self.r1):
            moved.wait_recv()
        add_into(self.quarter(0, None), [self.buf(1, None), self.buf(2, None)])
        self.c = []
        for k, d in enumerate((1, 3, 2)):
            there = self.net.moved(self.b, d)[self.b]
            self.c.append(
                self.net.copy(self.at(**{self.b: there, self.e: None}), self.mid.at[k], self.net.ring(self.b, d))
            )

    def p3(self):
        for moved in self.c:
            moved.wait_recv()
        add_into(self.at(**{self.e: None}), [self.mid.at[k] for k in range(3)])
        self.c = []
        for k, d in enumerate((1, 3, 2)):
            there = self.net.moved(self.e, d)[self.e]
            self.c.append(self.net.copy(self.at(**{self.e: there}), self.low.at[k], self.net.ring(self.e, d)))

    def result(self):
        for moved in self.c:
            moved.wait_recv()
        value = self.at()[...].astype(F32)
        for k in range(3):
            value = value + self.low[k].astype(F32)
        return value


RECTS = (
    (5, (0, 16), 512, 0, 512, 0),
    (5, (16, 16), 512, 0, 512, 1),
    (5, (32, 32), 512, 0, 512, 2),
    (4, (0, 16), 2048, 0, 512, 0),
    (4, (0, 16), 2048, 512, 1024, 1),
    (4, (0, 16), 2048, 1536, 512, 2),
    (3, (0, 16), 512, 0, 512, 0),
    (0, (0, 16), 512, 0, 512, 0),
    (1, (0, 16), 512, 0, 512, 1),
    (2, (0, 16), 512, 0, 512, 2),
)
BIG_FIRST = tuple(tuple(reversed(o)) for o in ORDER)


def reduce_buffers():
    shapes = []
    for _, (_, rows), _, _, width, order in RECTS:
        a, b, e = BIG_FIRST[order]
        shapes += [
            CHIPS + (rows, width),
            (3,) + chip_shape((a,)) + (rows, width),
            (3,) + chip_shape((a, b)) + (rows, width),
            (3, rows, width),
        ]
    return shapes


class Return:
    def __init__(self, net, window, encoded, back, out, local_sem):
        self.net = net
        lo = lax.rem(net.me["y"], 2)
        other = 1 - lo
        self.lo = lo
        self.window, self.back = window, back
        self.plain = [
            (window.at[rows_at(HALO + TOK * other, TOK)], back.at[0, lo], net.pair(0, other)),
            (encoded.at[rows_at(TOK * other, TOK)], out.at[lo], net.pair(0, other)),
        ]
        self.local = pltpu.make_async_copy(encoded.at[rows_at(TOK * lo, TOK)], out.at[lo], local_sem)
        self.base = net.used
        net.used += 16

    def start(self):
        net, lo = self.net, self.lo
        self.plain = [net.copy(*p) for p in self.plain]
        self.local.start()
        self.copies = []
        for k in range(4):
            for q in range(2):
                by, rows, to, only = pieces(q)[k]
                if only is not None and only != q:
                    continue
                side = 1 if by == 1 else 2
                copy = net.make(
                    self.window.at[pl.ds(to, TOK // 2)],
                    self.back.at[side, lo, rows],
                    net.pair(-by, q),
                    self.base + 4 * k + q,
                    self.base + 4 * k + 2 + lo,
                )
                copy.start()
                self.copies.append(copy)

    def gets(self):
        net = self.net
        for copy in self.plain:
            copy.wait_recv()
        for k in range(4):
            _, rows, _, only = pieces(0)[k]
            for m in range(2):
                copy = net.make(
                    self.window.at[pl.ds(0, TOK // 2)],
                    self.back.at[1, m, rows],
                    net.pair(1, 0),
                    0,
                    self.base + 4 * k + 2 + m,
                )
                if only is None:
                    copy.wait_recv()
                else:
                    pl.when(self.lo == only)(copy.wait_recv)

    def total(self, token_grad):
        lo = self.lo
        half = TOK // 2
        own = self.window[rows_at(HALO + TOK * lo, TOK), :].astype(F32)
        for m in range(2):
            base = jnp.where(lo == m, own, self.back[0, m].astype(F32))
            right = self.back[1, m].astype(F32)
            left = self.back[2, m].astype(F32)
            low = base[:half] + left[:half] + jnp.where(lo == 1, right[:half], 0.0)
            high = base[half:] + right[half:] + jnp.where(lo == 0, left[half:], 0.0)
            token_grad[m] = jnp.concatenate([low, high], axis=0).astype(BF)

    def finish(self):
        self.local.wait()
        for copy in self.copies:
            copy.wait_send()


def reduce_kernel(*refs):
    grads, (window_hbm, encoded) = refs[:6], refs[6:8]
    outs, out, token_grad = refs[8:14], refs[14], refs[15]
    rest = refs[16:]
    full, rest = rest[:6], rest[6:]
    bufs, rest = rest[:40], rest[40:]
    window, back = rest[:2]
    finals, rest = rest[2:8], rest[8:]
    ends, rest = rest[:6], rest[6:]
    send_sem, recv_sem, local_sem = rest
    net = Net(send_sem, recv_sem)
    c = net.me["c"]
    loads = [pltpu.make_async_copy(g, f, local_sem.at[k]) for k, (g, f) in enumerate(zip(grads, full))]
    loads.append(pltpu.make_async_copy(window_hbm, window, local_sem.at[6]))
    for load in loads:
        load.start()
    net.barrier()
    for load in loads:
        load.wait()
    lanes = []
    for k, (w, (r0, rows), per_core, base, width, order) in enumerate(RECTS):
        lanes.append(
            Reduce(
                net,
                full[w],
                pl.ds(r0, rows),
                c * per_core + base,
                width,
                (1 - c) * per_core + base,
                BIG_FIRST[order],
                bufs[4 * k : 4 * k + 4],
            )
        )
    each(lanes, "d0")
    back_rows = Return(net, window, encoded, back, out, local_sem.at[7])
    back_rows.start()
    first, second, third = lanes[:3], lanes[3:6], lanes[6:]
    each(first, "p1")
    each(second, "p1")
    each(first, "p1_mid")
    each(third, "p1")
    each(first, "p2")
    each(second, "p1_mid")
    each(first, "p3")
    each(third, "p1_mid")
    each(second, "p2")
    each(third, "p2")
    each(second, "p3")
    each(third, "p3")
    for lane, (w, (r0, rows), per_core, base, width, _) in zip(lanes, RECTS):
        finals[w][pl.ds(r0, rows), pl.ds(base, width)] = lane.result()
    swaps = []
    for w in range(6):
        n = finals[w].shape[0] // 2
        width = finals[w].shape[1]
        kept = finals[w].at[pl.ds(pl.multiple_of(n * c, 8), n)]
        given = finals[w].at[pl.ds(pl.multiple_of(n * (1 - c), 8), n)]
        swaps.append(net.copy(given, ends[w].at[:, columns(c * width, width)], net.ring("c", 0)))
        ends[w][:, columns(c * width, width)] = kept[...]
    back_rows.gets()
    back_rows.total(token_grad)
    for swap in swaps:
        swap.wait_recv()
    stores = [pltpu.make_async_copy(e, o, local_sem.at[k]) for k, (e, o) in enumerate(zip(ends, outs))]
    for store in stores:
        store.start()
    for store in stores:
        store.wait()
    back_rows.finish()
    net.finish()


def reduce_all(grads, window, encoded):
    any_space = pl.BlockSpec(memory_space=pl.ANY)
    full = [CHIPS + s for s in BLOCKS]
    owned = [(r // 2, n) for r, n in BLOCKS]
    return pl.pallas_call(
        reduce_kernel,
        name="reduce_all",
        out_shape=[jax.ShapeDtypeStruct(s, F32) for s in owned]
        + [jax.ShapeDtypeStruct((2, TOK, D), BF), jax.ShapeDtypeStruct((2, TOK, D), BF)],
        in_specs=[any_space] * 8,
        out_specs=[any_space] * 7 + [pl.BlockSpec(memory_space=pltpu.VMEM)],
        scratch_shapes=[pltpu.VMEM(s, BF) for s in full]
        + [pltpu.VMEM(s, BF) for s in reduce_buffers()]
        + [pltpu.VMEM((WIN, D), BF), pltpu.VMEM((3, 2, TOK, D), BF)]
        + [pltpu.VMEM((r, n // 2), F32) for r, n in BLOCKS]
        + [pltpu.VMEM(s, F32) for s in owned]
        + [
            pltpu.SemaphoreType.DMA((N_SEM,)),
            pltpu.SemaphoreType.DMA((N_SEM,)),
            pltpu.SemaphoreType.DMA((8,)),
        ],
        compiler_params=pltpu.CompilerParams(collective_id=2, has_side_effects=True, vmem_limit_bytes=62 << 20),
    )(*grads, window, encoded)


def dot(a, b):
    return jnp.dot(a, b, preferred_element_type=F32)


def norm(a, gain, shift):
    centred = a - jnp.mean(a, axis=-1, keepdims=True)
    inv = lax.rsqrt(jnp.mean(centred * centred, axis=-1, keepdims=True) + 1e-05)
    n = centred * inv
    return n * gain + shift, n, inv


def norm_back(d, n, inv, gain):
    dn = d * gain
    da = inv * (dn - jnp.mean(dn, axis=-1, keepdims=True) - n * jnp.mean(dn * n, axis=-1, keepdims=True))
    return da, jnp.sum(d * n, axis=0), jnp.sum(d, axis=0)


def segments(lengths, order, start, count):
    ends = jnp.cumsum(jnp.take(lengths, order))
    at = start + jnp.arange(count)
    segment = jnp.sum((ends[:, None] <= at[None, :]).astype(jnp.int32), axis=0)
    return jnp.where(at < 0, -1, segment)


def layer(window, cots, segment, full, vectors):
    wq, wk, wv, wo, wi, wu = full
    bq, bv, bo, g1, s1, bu, g2, s2, bi = [v.astype(F32) for v in vectors]
    rows = window[HALO : HALO + OWN]
    q = (dot(rows, wq) + bq).astype(BF).reshape(OWN, HEADS, HEAD)
    k = dot(window, wk).astype(BF).reshape(WIN, HEADS, HEAD)
    v = (dot(window, wv) + bv).astype(BF).reshape(WIN, HEADS, HEAD)
    same = (segment[HALO : HALO + OWN, None] == segment[None, :])[None]
    scores = jnp.einsum("qhd,khd->hqk", q, k, preferred_element_type=F32) * 0.125
    scores = jnp.where(same, scores, -1e30)
    e = jnp.exp(scores - jnp.max(scores, axis=-1, keepdims=True))
    probs = e / jnp.sum(e, axis=-1, keepdims=True)
    low = probs.astype(BF)
    mixed = jnp.einsum("hqk,khd->qhd", low, v, preferred_element_type=F32)
    context = mixed.reshape(OWN, D).astype(BF)
    attended = rows.astype(F32) + (dot(context, wo) + bo)
    normed, n1, inv1 = norm(attended, g1, s1)
    normed_low = normed.astype(BF)
    pre = dot(normed_low, wi) + bi
    phi = 0.5 * (1.0 + lax.erf(pre * math.sqrt(0.5)))
    activated = (pre * phi).astype(BF)
    slope = phi + pre * jnp.exp(-0.5 * pre * pre) * (1.0 / math.sqrt(2 * math.pi))
    encoded, n2, inv2 = norm(normed + (dot(activated, wu) + bu), g2, s2)
    d_final, dg2, ds2 = norm_back(cots.astype(F32), n2, inv2, g2)
    d_outer = d_final.astype(BF)
    tdot = lambda a, b: lax.dot_general(a, b, (((0,), (0,)), ((), ())), preferred_element_type=F32)
    dott = lambda a, b: lax.dot_general(a, b, (((1,), (1,)), ((), ())), preferred_element_type=F32)
    gwu = tdot(activated, d_outer).astype(BF)
    dbu = jnp.sum(d_outer.astype(F32), axis=0)
    d_inner = (dott(d_outer, wu) * slope).astype(BF)
    gwi = tdot(normed_low, d_inner).astype(BF)
    dbi = jnp.sum(d_inner.astype(F32), axis=0)
    d_normed = d_final + dott(d_inner, wi)
    d_attended, dg1, ds1 = norm_back(d_normed, n1, inv1, g1)
    d_branch = d_attended.astype(BF)
    gwo = tdot(context, d_branch).astype(BF)
    dbo = jnp.sum(d_branch.astype(F32), axis=0)
    d_context = dott(d_branch, wo).astype(BF)
    dc = d_context.reshape(OWN, HEADS, HEAD)
    dv = jnp.einsum("hqk,qhd->khd", low, dc, preferred_element_type=F32).reshape(WIN, D).astype(BF)
    dp = jnp.einsum("qhd,khd->hqk", dc, v, preferred_element_type=F32)
    dsum = jnp.sum((d_context.astype(F32) * context.astype(F32)).reshape(OWN, HEADS, HEAD), axis=-1)
    dr = (probs * (dp - dsum.T[:, :, None]) * 0.125).astype(BF)
    dq = jnp.einsum("hqk,khd->qhd", dr, k, preferred_element_type=F32).reshape(OWN, D).astype(BF)
    dk = jnp.einsum("hqk,qhd->khd", dr, q, preferred_element_type=F32).reshape(WIN, D).astype(BF)
    gwq = tdot(rows, dq).astype(BF)
    gwk = tdot(window, dk).astype(BF)
    gwv = tdot(window, dv).astype(BF)
    dbq = jnp.sum(dq.astype(F32), axis=0)
    dbv = jnp.sum(dv.astype(F32), axis=0)
    dx = dott(dk, wk) + dott(dv, wv)
    mid = dx[HALO : HALO + OWN] + d_attended + dott(dq, wq)
    dx = jnp.concatenate([dx[:HALO], mid, dx[HALO + OWN :]], axis=0).astype(BF)
    grads = (gwq, gwk, gwv, gwo, gwi, gwu)
    return encoded.astype(BF), dx, grads, (dbq, dbv, dbo, dg1, ds1, dbu, dg2, ds2, dbi)


def local(
    tokens, cotangent, seq_lengths, block_offsets, deal_order, wq, wk, wv, wo, bq, bv, bo, g1, s1, wi, bi, wu, bu, g2, s2
):
    lo = lax.rem(lax.axis_index("dp"), 2)
    own = jnp.concatenate([wq, wk, wv, wo] + [wi[:, D * j : D * j + D] for j in range(4)] + [wu], axis=0)
    gathered = gather_all(own, tokens[:, 0], cotangent[:, 0])
    full = [w.reshape(-1, w.shape[-1]) for w in gathered[:6]]
    window, cots = gathered[6:]
    small = jnp.concatenate([bq, bv, bo, g1, s1, bu, g2, s2, bi])
    both = lax.all_gather(small, ("dp", "shard"), axis=0)
    vectors = [both[:, 8 * j : 8 * j + 8].reshape(-1) for j in range(8)] + [both[:, 64:].reshape(-1)]
    lengths = lax.dynamic_index_in_dim(seq_lengths[:, 0], lo, 0, keepdims=False)
    order = lax.dynamic_index_in_dim(deal_order[:, 0], lo, 0, keepdims=False)
    start = lax.div(lax.axis_index("dp"), 2) * OWN - HALO
    segment = segments(lengths, order, start, WIN)
    encoded, dx, grads, small_grads = layer(window, cots, segment, full, vectors)
    blocked = [g.reshape(CHIPS + s) for g, s in zip(grads, BLOCKS)]
    *owned, out, token_grad = reduce_all(blocked, dx, encoded)
    lines = jnp.concatenate([g.reshape(128, -1) for g in small_grads], axis=1)
    mine = lax.psum_scatter(lines, ("dp", "shard"), scatter_dimension=0, tiled=True)[0]
    sbq, sbv, sbo, sg1, ss1, sbu, sg2, ss2 = [mine[8 * j : 8 * j + 8] for j in range(8)]
    return (out[:, None], token_grad[:, None], *owned[:4], sbq, sbv, sbo, sg1, ss1, owned[4], mine[64:], owned[5], sbu, sg2, ss2)


def solution(mesh):
    rows = P(None, "shard", "dp", None)
    table = P(None, "shard", None)
    matrix, vector = P(("dp", "shard"), None), P(("dp", "shard"))
    in_specs = (rows, rows) + (table,) * 3 + (matrix,) * 4 + (vector,) * 5 + (matrix, vector, matrix) + (vector,) * 3
    out_specs = (rows, rows) + (matrix,) * 4 + (vector,) * 5 + (matrix, vector, matrix) + (vector,) * 3
    return jax.shard_map(local, mesh=mesh, in_specs=in_specs, out_specs=out_specs, check_vma=False)
```

time: 1540 us -> 491 us (0.32)
  waiting for transfers between devices: 827 us -> 0 us
  local copies, waits for them, and re-layouts: 352 us -> 55.2 us
  Pallas kernels: 0 us -> 184 us
  matrix products: 218 us -> 99.9 us
  blocking collectives: 83.8 us -> 128 us
    all_gather x6 -> x0, waiting for transfers between devices: 494 us -> none  [the longest x2 414 us: side_by_side(): lax.all_gather(both, axis, axis=dim, tiled=True)]
    unnamed x8 -> x0, waiting for transfers between devices: 333 us -> none
    pallas_call x0 -> x2, Pallas kernels: none -> 184 us  [the longest x1 95.5 us: gather_all(): pl.pallas_call(gather_kernel, name='gather_all', out_shape=[jax.ShapeDtyp...]
    dot_general x48 -> x23, matrix products: 218 us -> 90.8 us  [the longest x6 29 us: dot(): return jnp.dot(a, b, preferred_element_type=F32)]
    unnamed x292 -> x75, local copies, waits for them, and re-layouts: 148 us -> 22.2 us
    another operation x8 -> x0, local copies, waits for them, and re-layouts: 57.3 us -> none  [the longest x6 57.1 us: sum_packed(): lines = jnp.concatenate([b.reshape(peers, -1) for b in parts], axis=1)]
    unnamed x1 -> x2, blocking collectives: 83.8 us -> 128 us
    reshape x14 -> x9, local copies, waits for them, and re-layouts: 43.6 us -> 7.85 us  [local(): lines = jnp.concatenate([g.reshape(128, -1) for g in small_grads], axis=1)]
  transfers between devices with their start and end apart: 7 -> 0, of which waited for: 4 -> 0; matrix products, arithmetic and copies ran while one was open for 28% -> 0% of each run, Pallas kernels for 0% -> 0%
where the time goes in v1:
time: 491 us; the launch traced here: 486 us
  Pallas kernels  184 us (37%)
  blocking collectives  128 us (26%)
  matrix products  99.9 us (20%)
  local copies, waits for them, and re-layouts  55.2 us (11%)
  other arithmetic  17.6 us (4%)
    unnamed x2, blocking collectives  128 us
    pallas_call x1, Pallas kernels, gather_all(): pl.pallas_call(gather_kernel, name='gather_all', out_shape=[jax.ShapeDtyp...  95.5 us
    pallas_call x1, Pallas kernels, reduce_all(): pl.pallas_call(reduce_kernel, name='reduce_all', out_shape=[jax.ShapeDtyp...  88.3 us
    dot_general x6, matrix products, dot(): return jnp.dot(a, b, preferred_element_type=F32)  29 us
    unnamed x75, local copies, waits for them, and re-layouts  22.2 us
    dot_general x6, matrix products, layer(): lax.dot_general(a, b, (((0,), (0,)), ((), ())), preferred_element_type=F32)  22.1 us
    dot_general x6, matrix products, layer(): lax.dot_general(a, b, (((1,), (1,)), ((), ())), preferred_element_type=F32)  18.2 us

profile of v1, /device:TPU:1, one launch (start us, length us, event | category | flops | bytes accessed | tf_op | source)
XLA Modules:
  0.0 485.8 jit_solution(306431675587483393)
XLA Ops:
  12.0 95.5 %gather_all.1 = (bf16[4,2,2,4,16,1024]{5,4,3,2,1,0:T(8,128)(2,1)}, bf16[4,2,2,4,16,1024]{5,4,3,2,1,0:T(8,128)(2,1)}, bf16[4,2,2,4,16,1024]{5,4,3,2,1,0:T(8,128)(...) custom-call(bf16[96,1024]{1,0:T(8,128)(2,1)S(1)} %constant_dynamic-u, ...), custom_call_target="tpu_custom_call" | custom-call | tf_op jit(solution)/shard_map/gather_all/pallas_call | solution.py:357
  107.5 6.1 %concatenate.14 = bf16[96]{0:T(256)(128)(2,1)S(1)} concatenate(bf16[8]{0:T(256)(128)(2,1)} %param.28, bf16[8]{0:T(256)(128)(2,1)} %param.29, bf16[8]{0:T(256)(128)(2,1)} %param.30, bf16[8]{0:T(256)(128)(2,1)} %param.31, bf16[8]{0:T(256)(128)(2,1)} %param.32, bf16[8]{0:T(256)(128)(2,1)} %param.36, bf16[8]{0:T(256)(128)(2,1)} %param.37, bf16[8]{0:T(256)(128)(2,1)} %param.38, ...), dimensions={0} | concatenate | bytes 384 | tf_op jit(solution)/shard_map/concatenate | solution.py:755
  113.8 65.1 %all-reduce = bf16[12288]{0:T(1024)(128)(2,1)S(1)} all-reduce(bf16[12288]{0:T(1024)(128)(2,1)S(1)} %dynamic-update-slice), channel_id=2, replica_groups=mesh['dp'=8,'shard'=16] {'dp','shard'}, use_global_device_ids=true, to_apply=%add | all-reduce | flops 12288 | bytes 49152
  182.5 4.5 convolution_convert_fusion.8
  189.4 9.2 %fusion.38 = (f32[16,256]{1,0:T(8,128)S(1)}, f32[16,256,640]{2,1,0:T(8,128)}) fusion(pred[256,640]{1,0:T(8,128)(4,1)S(1)} %broadcast_compare_fusion, bf16[256,16,64]{0,2,1:T(8,128)(2,1)S(1)} %bitcast.132, bf16[640,16,64]{0,2,1:T(8,128)(2,1)} %bitcast.126), kind=kOutput, calls=%fused_computation.129 | convolution fusion | flops 346030720 | bytes 12500992 | tf_op jit(solution)/shard_map/sub | solution.py:700
  198.6 7.3 %fusion.6 = bf16[16,256,640]{2,1,0:T(8,128)(2,1)} fusion(f32[16,256,640]{2,1,0:T(8,128)} %get-tuple-element.149, f32[16,256]{1,0:T(8,128)S(1)} %get-tuple-element.148), kind=kLoop, calls=%fused_computation.16 | loop fusion | flops 5242880 | bytes 15745024 | tf_op jit(solution)/shard_map/convert_element_type | solution.py:702
  205.9 4.3 add_convert_fusion
  212.7 4.6 convolution_convert_fusion.10
  222.2 8.9 %multiply_convert_fusion.1 = (bf16[256,4096]{1,0:T(8,128)(2,1)}, f32[256,4096]{1,0:T(8,128)}) fusion(f32[4096]{0:T(1024)S(1)} %reshape.402, bf16[1024,4096]{1,0:T(8,128)(2,1)} %bitcast.145, f32[256,1024]{1,0:T(8,128)S(1)} %get-tuple-element.151, f32[1024]{0:T(1024)S(1)} %reshape.401, f32[1024]{0:T(1024)S(1)} %reshape.400, f32[256]{0:T(256)S(1)} %add_rsqrt_fusion.1, ...), kind=kOutput, calls=%fused_computation.22 | convolution fusion | flops 2155085824 | bytes 15755264 | tf_op jit(solution)/shard_map/dot_general | solution.py:667
  231.2 6.5 %fusion.40 = (f32[256]{0:T(256)S(1)}, f32[256,1024]{1,0:T(8,128)S(1)}) fusion(f32[1024]{0:T(1024)S(1)} %reshape.403, bf16[256,4096]{1,0:T(8,128)(2,1)} %get-tuple-element.152, bf16[4096,1024]{1,0:T(8,128)(2,1)} %bitcast.149, f32[1024]{0:T(1024)S(1)} %reshape.401, f32[1024]{0:T(1024)S(1)} %reshape.400, f32[256]{0:T(256)S(1)} %add_rsqrt_fusion.1, ...), kind=kOutput, calls=%fused_computation.131 | convolution fusion | flops 2149318400 | bytes 12598272 | tf_op jit(solution)/shard_map/dot_general | solution.py:667
  239.2 3.2 fusion.23
  243.4 7.9 %convert_reduce_fusion = (f32[4096]{0:T(1024)}, bf16[256,4096]{1,0:T(8,128)(2,1)S(1)}) fusion(f32[256,4096]{1,0:T(8,128)} %get-tuple-element.153, bf16[4096,1024]{1,0:T(8,128)(2,1)} %bitcast.150, f32[256,1024]{1,0:T(8,128)S(1)} %get-tuple-element.126), kind=kOutput, calls=%fused_computation.21 | convolution fusion | flops 2160324608 | bytes 15745024 | tf_op jit(solution)/shard_map/dot_general | solution.py:716
  251.3 2.8 multiply_reduce_fusion
  256.5 3.6 convert_multiply_fusion.2
  262.1 4.7 convert_reduce_fusion.1
  266.9 2.5 copy.72
  270.8 5.9 %multiply_convert_fusion = bf16[16,256,640]{2,1,0:T(8,128)(2,1)S(1)} fusion(f32[16,256]{1,0:T(8,128)S(1)} %bitcast.144, f32[16,256,640]{2,1,0:T(8,128)} %get-tuple-element.149, f32[16,256]{1,0:T(8,128)S(1)} %copy-done.23, bf16[256,16,64]{0,2,1:T(8,128)(2,1)} %bitcast.137, bf16[640,16,64]{0,2,1:T(8,128)(2,1)} %bitcast.125), kind=kOutput, calls=%fused_computation.2 | convolution fusion | flops 348651520 | bytes 17596416 | tf_op jit(solution)/shard_map/qhd,khd->hqk/dot_general | solution.py:730
  288.9 62.9 %all-reduce.1 = f32[128,96]{1,0:T(8,128)S(1)} all-reduce(f32[128,96]{1,0:T(8,128)} %concatenate.16), channel_id=3, replica_groups=mesh['dp'=8,'shard'=16] {'dp','shard'}, use_global_device_ids=true, to_apply=%region_22.23.clone | all-reduce | flops 12288 | bytes 98304
  353.0 3.7 convolution_convert_fusion.7
  363.7 5.6 %convolution_convert_fusion = bf16[4096,1024]{1,0:T(8,128)(2,1)} fusion(bf16[256,4096]{1,0:T(8,128)(2,1)S(1)} %copy-done.13, f32[256,1024]{1,0:T(8,128)S(1)} %copy-done.12), kind=kOutput, calls=%fused_computation.6 | convolution fusion | flops 2151940096 | bytes 11534336 | tf_op jit(solution)/shard_map/dot_general | solution.py:715
  369.3 5.8 %convolution_convert_fusion.1 = bf16[1024,4096]{1,0:T(8,128)(2,1)} fusion(bf16[256,4096]{1,0:T(8,128)(2,1)S(1)} %copy-done.15, f32[256,1024]{1,0:T(8,128)S(1)} %get-tuple-element.151, f32[1024]{0:T(1024)S(1)} %reshape.401, f32[1024]{0:T(1024)S(1)} %reshape.400, f32[256]{0:T(256)S(1)} %add_rsqrt_fusion.1, f32[256]{0:T(256)S(1)} %broadcast_multiply_fusion.5), kind=kOutput, calls=%fused_computation.7 | convolution fusion | flops 2152988672 | bytes 11544576 | tf_op jit(solution)/shard_map/dot_general | solution.py:715
  377.1 3.4 convolution_convert_fusion.4
  380.5 3.1 convolution_convert_fusion.5
  385.7 88.3 %reduce_all.1 = (f32[8,1024]{1,0:T(8,128)}, f32[8,1024]{1,0:T(8,128)}, f32[8,1024]{1,0:T(8,128)}, f32[8,1024]{1,0:T(8,128)}, f32[8,4096]{1,0:T(8,128)}, /*index=...) custom-call(bf16[4,2,2,4,16,1024]{5,4,3,2,1,0:T(8,128)(2,1)} %bitcast.121, ...), custom_call_target="tpu_custom_call" | custom-call | tf_op jit(solution)/shard_map/reduce_all/pallas_call | solution.py:645
  (141 shorter events, 69.2 us)
Async XLA Ops:
  182.5 6.9 %copy-start.16 = (bf16[256,1024]{0,1:T(8,128)(2,1)}, bf16[256,1024]{0,1:T(8,128)(2,1)S(1)}, u32[]{:S(2)}) copy-start(bf16[256,1024]{0,1:T(8,128)(2,1)S(1)} %copy.68) | copy-start | bytes 1572868
  198.6 7.3 %copy-start.22 = (f32[16,256]{1,0:T(8,128)}, f32[16,256]{1,0:T(8,128)S(1)}, u32[]{:S(2)}) copy-start(f32[16,256]{1,0:T(8,128)S(1)} %get-tuple-element.148) | copy-start | bytes 49156
  217.3 2.9 copy-start.7
  222.2 8.9 %copy-start.20 = (f32[128,8]{1,0:T(8,128)S(1)}, f32[128,8]{1,0:T(8,128)}, u32[]{:S(2)}) copy-start(f32[128,8]{1,0:T(8,128)} %get-tuple-element.134) | copy-start | bytes 12292
  231.2 7.8 %copy-start.19 = (f32[128,8]{1,0:T(8,128)S(1)}, f32[128,8]{1,0:T(8,128)}, u32[]{:S(2)}) copy-start(f32[128,8]{1,0:T(8,128)} %get-tuple-element.133) | copy-start | bytes 12292
  239.2 3.2 copy-start.6
  242.5 8.8 %slice-start = ((s8[8388608]{0:T(1024)(128)(4,1)}), s8[4194304]{0:T(1024)(128)(4,1)S(1)}, s32[]{:S(2)}) async-start(s8[8388608]{0:T(1024)(128)(4,1)} %bitcast.146), calls=%async_computation | async-start | bytes 8388608
  243.4 7.9 %copy-start.11 = (f32[256,1024]{1,0:T(8,128)}, f32[256,1024]{1,0:T(8,128)S(1)}, u32[]{:S(2)}) copy-start(f32[256,1024]{1,0:T(8,128)S(1)} %get-tuple-element.126) | copy-start | bytes 3145732
  243.4 7.9 %slice-start.1 = ((s8[8388608]{0:T(1024)(128)(4,1)}), s8[4194304]{0:T(1024)(128)(4,1)S(1)}, s32[]{:S(2)}) async-start(s8[8388608]{0:T(1024)(128)(4,1)} %bitcast.146), calls=%async_computation.1 | async-start | bytes 8388608
  251.3 2.8 copy-start.14
  266.8 3.9 copy-start.23
  270.8 5.9 %copy-start.9 = (bf16[640,1024]{0,1:T(8,128)(2,1)S(1)}, bf16[640,1024]{0,1:T(8,128)(2,1)}, u32[]{:S(2)}) copy-start(bf16[640,1024]{0,1:T(8,128)(2,1)} %copy.66) | copy-start | bytes 3932164
  276.7 2.5 copy-start.4
  353.0 3.7 copy-start.25
  356.7 1.6 copy-start.18
  356.7 2.0 copy-start.24
  358.7 1.6 copy-start.10
  358.7 1.8 copy-start.17
  361.3 1.5 copy-start.12
  361.3 2.4 copy-start.13
  363.7 5.6 %copy-start.15 = (bf16[256,4096]{1,0:T(8,128)(2,1)S(1)}, bf16[256,4096]{1,0:T(8,128)(2,1)}, u32[]{:S(2)}) copy-start(bf16[256,4096]{1,0:T(8,128)(2,1)} %copy-done.14) | copy-start | bytes 6291460
  369.3 5.8 %copy-start.8 = (bf16[16,64,256]{2,1,0:T(8,128)(2,1)S(1)}, bf16[16,64,256]{2,1,0:T(8,128)(2,1)}, u32[]{:S(2)}) copy-start(bf16[16,64,256]{2,1,0:T(8,128)(2,1)} %copy-done.7) | copy-start | bytes 1572868
  385.7 99.8 %copy-start.1 = (s32[2,1,16]{2,1,0:T(1,128)S(1)}, s32[2,1,16]{2,1,0:T(1,128)}, u32[]{:S(2)}) copy-start(s32[2,1,16]{2,1,0:T(1,128)} %param.22) | copy-start | bytes 388
  474.1 10.8 %copy-start.21 = (f32[32,1024]{1,0:T(8,128)S(1)}, f32[32,1024]{1,0:T(8,128)}, u32[]{:S(2)}) copy-start(f32[32,1024]{1,0:T(8,128)} %get-tuple-element.199) | copy-start | bytes 393220
  (4 other events, 3.8 us)

commit v2 on v1

--- a/solution.py
+++ b/solution.py
@@ -290,22 +290,211 @@
     full[5][here + (slice(None), half)] = both(mine[64:96, half], peer[64:96, half])
 
 
-def gather_kernel(own, tokens, cotangent, *refs):
-    outs, rest = refs[:8], refs[8:]
-    mine, peer = rest[:2]
-    full = rest[2:8]
-    send_sem, recv_sem, local_sem = rest[8:]
+BLOCKS = ((16, 1024),) * 4 + ((16, 4096), (64, 1024))
+
+
+SPAN = TOK + 2 * HALO
+NT = (((1,), (1,)), ((), ()))
+TN = (((0,), (0,)), ((), ()))
+NN = (((1,), (0,)), ((), ()))
+
+
+def mm(a, b, dims=NN):
+    return lax.dot_general(a, b, dims, preferred_element_type=F32)
+
+
+def tile(w, n0, n):
+    return w[:, :, :, :, :, columns(n0, n)].reshape(-1, n)
+
+
+def project(rows, w, out, bias=None, n=512):
+    def body(t, carry):
+        cols = columns(t * n, n)
+        y = mm(rows[...], tile(w, t * n, n))
+        if bias is not None:
+            y = y + bias[:, cols]
+        out[:, cols] = y.astype(BF)
+        return carry
+
+    lax.fori_loop(0, out.shape[1] // n, body, 0)
+
+
+def lane_split(x):
+    low = lax.broadcasted_iota(jnp.int32, x.shape, 1) < HEAD
+    zero = jnp.zeros_like(x)
+    return jnp.concatenate([jnp.where(low, x, zero), jnp.where(low, zero, x)], axis=0)
+
+
+def lane_join(x):
+    n = x.shape[0] // 2
+    low = lax.broadcasted_iota(jnp.int32, (n, x.shape[1]), 1) < HEAD
+    return jnp.where(low, x[:n], x[n:])
+
+
+def attention(q, k, v, bias, probs, context, first, last):
+    def body(h, carry):
+        cols = columns(h * 128, 128)
+        for b in range(2):
+            mine, near = pl.ds(b * TOK, TOK), pl.ds(b * TOK, SPAN)
+            pen = bias[b]
+            s = mm(k[near, cols], lane_split(q[mine, cols]), NT) * 0.125 + jnp.concatenate([pen, pen], axis=1)
+            e = jnp.exp(s - jnp.max(s, axis=0, keepdims=True))
+            p = (e * (1.0 / jnp.sum(e, axis=0, keepdims=True))).astype(BF)
+            at = columns((2 * h + b) * OWN, OWN)
+            probs[0, :, at], probs[1, :, at] = p[:OWN], p[OWN:]
+            y = mm(v[near, cols], p, TN)
+            y = jnp.concatenate([y[:HEAD, :TOK], y[HEAD:, TOK:]], axis=0)
+            context[mine, cols] = y.T.astype(BF)
+        return carry
+
+    lax.fori_loop(first, last, body, 0)
+
+
+def normalized(a):
+    centred = a - jnp.mean(a, axis=-1, keepdims=True)
+    inv = lax.rsqrt(jnp.mean(centred * centred, axis=-1, keepdims=True) + 1e-05)
+    return centred * inv, inv
+
+
+def norm_back(dn, n, inv):
+    return inv * (dn - jnp.mean(dn, axis=-1, keepdims=True) - n * jnp.mean(dn * n, axis=-1, keepdims=True))
+
+
+def feed_in(low, wi, bi, act, slope, first, last, n=512):
+    def body(t, carry):
+        cols = columns(t * n, n)
+        u = mm(low[...], tile(wi, t * n, n)) + bi[:, cols]
+        phi = 0.5 + 0.5 * lax.erf(u * math.sqrt(0.5))
+        act[:, cols] = (u * phi).astype(BF)
+        slope[:, cols] = (phi + u * (jnp.exp(-0.5 * (u * u)) * (1.0 / math.sqrt(2 * math.pi)))).astype(BF)
+        return carry
+
+    lax.fori_loop(first, last, body, 0)
+
+
+ROWS = 32
+
+
+def some_rows(t):
+    return pl.ds(pl.multiple_of(t * ROWS, ROWS), ROWS)
+
+
+def segment_bias(lengths, order, start, lo, bias):
+    ends, total = [], 0
+    for k in range(16):
+        total = total + lengths[lo, order[lo, k]]
+        ends.append(total)
+
+    def which(at):
+        found = jnp.where(at < 0, -1, 0)
+        for e in ends:
+            found = found + (at >= e).astype(jnp.int32)
+        return found
+
+    keys = which(start + lax.broadcasted_iota(jnp.int32, (WIN, TOK), 0))
+    queries = which(start + HALO + lax.broadcasted_iota(jnp.int32, (8, OWN), 1))[:1]
+    for b in range(2):
+        same = keys[b * TOK : b * TOK + SPAN] == queries[:, b * TOK : b * TOK + TOK]
+        bias[b] = jnp.where(same, 0.0, -1e30)
+
+
+class Vectors:
+    def __init__(self, net, small, tiles, vec, inner):
+        self.net, self.small = net, small
+        self.own, self.sib, self.tz, self.ty, self.tx = tiles
+        self.vec, self.inner = vec, inner
+
+    def around(self, axis, block):
+        return [self.net.copy(block, block, self.net.ring(axis, d)) for d in (1, 3, 2)]
+
+    def start(self):
+        sh = lax.axis_index("shard")
+        r = lax.broadcasted_iota(jnp.int32, (16, 128), 0)
+        i = lax.broadcasted_iota(jnp.int32, (16, 128), 1)
+        value = jnp.broadcast_to(self.small[0:1, :].astype(F32), (16, 128))
+        part = (i < 64) & (lax.shift_right_logical(i, 3) == r)
+        inner = (i >= 64) & (i < 96) & (r == 8 + lax.div(sh, 4))
+        picked = jnp.where(part | inner, value, 0.0).astype(BF)
+        i = lax.broadcasted_iota(jnp.int32, (128, 128), 0)
+        to = lax.broadcasted_iota(jnp.int32, (128, 128), 1)
+        place = jnp.where(i < 64, 8 * sh + (i & 7), 32 * lax.rem(sh, 4) + i - 64)
+        self.own[...] = mm(picked, jnp.where((place == to) & (i < 96), 1.0, 0.0).astype(BF)).astype(BF)
+        self.c = [self.net.copy(self.own, self.sib, self.net.ring("c", 0))]
+
+    def wait(self):
+        for moved in self.c:
+            moved.wait_recv()
+
+    def along_z(self):
+        self.wait()
+        z = self.net.me["z"]
+        self.tz[z] = self.own[...] + self.sib[...]
+        self.c = self.around("z", self.tz.at[z])
+
+    def along_y(self):
+        self.wait()
+        y = self.net.me["y"]
+        self.ty[y] = (self.tz[0] + self.tz[1]) + (self.tz[2] + self.tz[3])
+        self.c = self.around("y", self.ty.at[y])
+
+    def along_x(self):
+        self.wait()
+        x = self.net.me["x"]
+        self.tx[x, 0] = self.ty[0] + self.ty[2]
+        self.tx[x, 1] = self.ty[1] + self.ty[3]
+        self.c = self.around("x", self.tx.at[x])
+
+    def done(self):
+        self.wait()
+        for dp in range(8):
+            got = self.tx[dp // 2, dp % 2].astype(F32)
+            self.vec[:, 128 * dp : 128 * dp + 128] = got[:8]
+            for t in range(4):
+                at = 512 * dp + 128 * t
+                self.inner[:, at : at + 128] = got[8 + t : 9 + t]
+
+
+BQ, BV, BO, G1, S1, BU, G2, S2 = range(8)
+
+
+def forward_kernel(*refs):
+    tokens, cotangent, lengths, order, small = refs[:5]
+    own, refs = refs[5:11], refs[11:]
+    outs, refs = refs[:21], refs[21:]
+    weights_out, refs_out = outs[:6], outs[6:]
+    (x_out, q_out, k_out, v_out, probs_out, context_out, low_out, act_out, slope_out) = refs_out[:9]
+    (n1_out, inv1_out, d_final_out, encoded_out, vec_out, two_out) = refs_out[9:]
+    mine, peer = refs[:2]
+    full, refs = refs[2:8], refs[8:]
+    window, cots, q, k, v, probs, context, low, act, slope, bias, refs = *refs[:11], refs[11:]
+    n1, inv1, normed, total, encoded, vec, inner, two, refs = *refs[:8], refs[8:]
+    tiles, refs = refs[:5], refs[5:]
+    send_sem, recv_sem, local_sem = refs
     net = Net(send_sem, recv_sem)
-    c = net.me["c"]
-    load = pltpu.make_async_copy(own, mine, local_sem.at[0])
-    load.start()
+    me, c = net.me, net.me["c"]
+    lo = lax.rem(me["y"], 2)
+    stores = []
+
+    def store(src, dst):
+        move = pltpu.make_async_copy(src, dst, local_sem.at[2 + len(stores)])
+        move.start()
+        stores.append(move)
+
+    def both(src, dst):
+        net.copy(src, dst.at[c], net.ring("c", 0))
+        store(src, dst.at[c])
+        return net.sent[-1]
+
+    for j in range(4):
+        mine[8 * j : 8 * j + 8, :] = own[j][...]
+        mine[32 + 8 * j : 40 + 8 * j, :] = own[4][:, 1024 * j : 1024 * j + 1024]
+    mine[64:96, :] = own[5][...]
     net.barrier()
-    load.wait()
     swap = net.copy(mine, peer, net.ring("c", 0))
-    window = Window(net, tokens, cotangent, outs[6], outs[7], local_sem)
-    window.start()
+    vectors = Vectors(net, small, tiles, vec, inner)
+    vectors.start()
     swap.wait_recv()
-    place_own(net.me, mine, peer, full)
+    place_own(me, mine, peer, full)
     rows = slice(None)
     half = columns(c * 512, 512)
     wi, wu = full[4], full[5]
@@ -321,54 +510,155 @@
         Gather(net, wu, pl.ds(16, 16), half, ORDER[1]),
         Gather(net, wu, pl.ds(32, 32), half, ORDER[2]),
     ]
-    for step in ("p1", "p2"):
-        for lanes in (first, second, third):
-            each(lanes, step)
+    for lanes in (first, second, third):
+        each(lanes, "p1")
+    view = Window(net, tokens, cotangent, window, cots, local_sem)
+    view.start()
+    vectors.along_z()
+    segment_bias(lengths, order, me["x"] * OWN - HALO, lo, bias)
+    each(first, "p2")
+    vectors.along_y()
+    each(second, "p2")
+    each(third, "p2")
+    vectors.along_x()
     each(first, "p3")
     each(second, "p3")
     each(first, "p3_mid")
+    each(third, "p3")
     each(first, "p3_core")
-    each(third, "p3")
+    vectors.done()
+    view.done()
+    each(second, "p3_mid")
     each(first, "p3_end")
+    got_x = both(window, x_out)
     each(first, "done")
-    for step in ("p3_mid", "p3_core", "p3_end"):
-        each(second, step)
+    project(window.at[pl.ds(HALO, OWN)], full[0], q, vec.at[BQ : BQ + 1])
     each(third, "p3_mid")
+    project(window, full[1], k)
+    each(second, "p3_core")
+    project(window, full[2], v, vec.at[BV : BV + 1])
+    for j in range(3):
+        store(full[j], weights_out[j])
+    store(q, q_out)
+    store(k, k_out)
+    store(v, v_out)
+    attention(q, k, v, bias, probs, context, 0, 2)
+    each(second, "p3_end")
     each(third, "p3_core")
+    attention(q, k, v, bias, probs, context, 2, 5)
+    each(third, "p3_end")
+    attention(q, k, v, bias, probs, context, 5, 8)
+    got_context = both(context, context_out)
+    store(probs, probs_out)
     each(second, "done")
-    each(third, "p3_end")
+    store(full[3], weights_out[3])
+    store(full[4], weights_out[4])
+
+    def attend(t, carry):
+        cols = columns(t * 512, 512)
+        y = mm(context[...], tile(full[3], t * 512, 512)) + vec[BO : BO + 1, cols]
+        total[:, cols] = y + window[pl.ds(HALO, OWN), cols].astype(F32)
+        return carry
+
+    lax.fori_loop(0, 2, attend, 0)
+
+    def norm_one(t, carry):
+        r = some_rows(t)
+        n, inv = normalized(total[r, :])
+        n1[r, :] = n
+        inv1[r, :] = jnp.broadcast_to(inv, (ROWS, 128))
+        y = n * vec[G1 : G1 + 1, :] + vec[S1 : S1 + 1, :]
+        normed[r, :] = y
+        low[r, :] = y.astype(BF)
+        return carry
+
+    lax.fori_loop(0, OWN // ROWS, norm_one, 0)
+    got_low = both(low, low_out)
+    store(n1, n1_out)
+    store(inv1, inv1_out)
+    feed_in(low, wi, inner, act, slope, 0, FF // 512)
+    got_act = both(act, act_out)
+    store(slope, slope_out)
+    store(vec, vec_out)
     each(third, "done")
-    window.done()
-    stores = [pltpu.make_async_copy(w, o, local_sem.at[2 + k]) for k, (w, o) in enumerate(zip(full, outs))]
-    for store in stores:
-        store.start()
-    for store in stores:
-        store.wait()
-    window.finish()
+    store(full[5], weights_out[5])
+
+    def feed_out(t, carry):
+        cols = columns(t * 512, 512)
+        y = mm(act[...], tile(wu, t * 512, 512)) + vec[BU : BU + 1, cols]
+        total[:, cols] = y + normed[:, cols]
+        return carry
+
+    lax.fori_loop(0, 2, feed_out, 0)
+
+    def norm_two(t, carry):
+        r = some_rows(t)
+        n, inv = normalized(total[r, :])
+        gain = vec[G2 : G2 + 1, :]
+        encoded[r, :] = (n * gain + vec[S2 : S2 + 1, :]).astype(BF)
+        d = cots[r, :].astype(F32)
+        normed[r, :] = norm_back(d * gain, n, inv)
+        dn = jnp.sum((d * n).reshape(ROWS // 8, 8, D), axis=0)
+        return carry[0] + dn, carry[1] + jnp.sum(d.reshape(ROWS // 8, 8, D), axis=0)
+
+    zero = jnp.zeros((8, D), F32)
+    gain_sum, shift_sum = lax.fori_loop(0, OWN // ROWS, norm_two, (zero, zero))
+    two[0:1, :] = jnp.sum(gain_sum, axis=0, keepdims=True)
+    two[1:2, :] = jnp.sum(shift_sum, axis=0, keepdims=True)
+    two[2:8, :] = jnp.zeros((6, D), F32)
+    store(normed, d_final_out)
+    store(encoded, encoded_out)
+    store(two, two_out)
+    for got in (got_x, got_context, got_low, got_act):
+        got.wait_recv()
+    for move in stores:
+        move.wait()
+    view.finish()
     net.finish()
 
 
-BLOCKS = ((16, 1024),) * 4 + ((16, 4096), (64, 1024))
-
-
-def gather_all(own, tokens, cotangent):
+def forward_all(tokens, cotangent, lengths, order, small, own):
     any_space = pl.BlockSpec(memory_space=pl.ANY)
-    full = [CHIPS + s for s in BLOCKS]
+    vmem = pl.BlockSpec(memory_space=pltpu.VMEM)
+    smem = pl.BlockSpec(memory_space=pltpu.SMEM)
+    full = [(CHIPS + s, BF) for s in BLOCKS]
+    kept = [
+        ((2, WIN, D), BF),
+        ((OWN, D), BF),
+        ((WIN, D), BF),
+        ((WIN, D), BF),
+        ((2, OWN, FF), BF),
+        ((2, OWN, D), BF),
+        ((2, OWN, D), BF),
+        ((2, OWN, FF), BF),
+        ((OWN, FF), BF),
+        ((OWN, D), F32),
+        ((OWN, 128), F32),
+        ((OWN, D), F32),
+        ((OWN, D), BF),
+        ((8, D), F32),
+        ((8, D), F32),
+    ]
+    scratch = [((96, 1024), BF)] * 2 + full
+    scratch += [((WIN, D), BF), ((OWN, D), BF), ((OWN, D), BF), ((WIN, D), BF), ((WIN, D), BF)]
+    scratch += [((2, OWN, FF), BF), ((OWN, D), BF), ((OWN, D), BF), ((OWN, FF), BF), ((OWN, FF), BF)]
+    scratch += [((2, SPAN, TOK), F32), ((OWN, D), F32), ((OWN, 128), F32), ((OWN, D), F32), ((OWN, D), F32)]
+    scratch += [((OWN, D), BF), ((8, D), F32), ((1, FF), F32), ((8, D), F32)]
+    scratch += [((16, 128), BF)] * 2 + [((4, 16, 128), BF)] * 2 + [((4, 2, 16, 128), BF)]
     return pl.pallas_call(
-        gather_kernel,
-        name="gather_all",
-        out_shape=[jax.ShapeDtypeStruct(s, BF) for s in full + [(WIN, D), (OWN, D)]],
-        in_specs=[any_space] * 3,
-        out_specs=[any_space] * 8,
-        scratch_shapes=[pltpu.VMEM((96, 1024), BF)] * 2
-        + [pltpu.VMEM(s, BF) for s in full]
+        forward_kernel,
+        name="forward_all",
+        out_shape=[jax.ShapeDtypeStruct(s, t) for s, t in full + kept],
+        in_specs=[any_space] * 2 + [smem] * 2 + [vmem] * 7,
+        out_specs=[any_space] * 21,
+        scratch_shapes=[pltpu.VMEM(s, t) for s, t in scratch]
         + [
             pltpu.SemaphoreType.DMA((N_SEM,)),
             pltpu.SemaphoreType.DMA((N_SEM,)),
-            pltpu.SemaphoreType.DMA((8,)),
+            pltpu.SemaphoreType.DMA((32,)),
         ],
-        compiler_params=pltpu.CompilerParams(collective_id=1, has_side_effects=True, vmem_limit_bytes=50 << 20),
-    )(own, tokens, cotangent)
+        compiler_params=pltpu.CompilerParams(collective_id=1, has_side_effects=True, vmem_limit_bytes=62 << 20),
+    )(tokens, cotangent, lengths, order, small, *own)
 
 
 def add_into(dst, srcs):
@@ -391,38 +681,28 @@
 
 
 class Reduce:
-    def __init__(self, net, ref, rows, base, width, other_base, order, bufs):
-        self.net, self.ref, self.rows, self.width = net, ref, rows, width
-        self.mine, self.theirs = columns(base, width), columns(other_base, width)
+    def __init__(self, net, ref, rows, cols, order, bufs):
+        self.net, self.ref, self.rows, self.cols = net, ref, rows, cols
         self.a, self.b, self.e = order
-        self.sib, self.wide, self.mid, self.low = bufs
-
-    def at(self, cols=None, **over):
+        self.wide, self.mid, self.low = bufs
+
+    def at(self, **over):
         place = {k: self.net.me[k] for k in AXES}
         place.update(over)
-        return self.ref.at[chip_index(place) + (self.rows, self.mine if cols is None else cols)]
-
-    def near(self, by):
-        return self.net.moved(self.a, by)[self.a]
+        return self.ref.at[chip_index(place) + (self.rows, self.cols)]
 
     def quarter(self, by, h):
         b = None if h is None else ("half", h)
-        return self.at(**{self.a: self.near(by), self.b: b, self.e: None})
+        return self.at(**{self.a: self.net.moved(self.a, by)[self.a], self.b: b, self.e: None})
 
     def buf(self, k, h):
         b = None if h is None else ("half", h)
         return self.wide.at[(k,) + chip_index({self.b: b, self.e: None}, drop=(self.a,))]
 
-    def d0(self):
-        every = {k: None for k in AXES}
-        self.c = self.net.copy(self.at(cols=self.theirs, **every), self.sib, self.net.ring("c", 0))
-
     def send(self, by, h, k, to):
         return self.net.copy(self.quarter(by, h), self.buf(k, h), self.net.ring(self.a, to))
 
     def p1(self):
-        self.c.wait_recv()
-        add_into(self.at(**{k: None for k in AXES}), [self.sib])
         self.m0 = self.send(2, 0, 0, 1)
         self.m1 = self.send(2, 1, 0, 3)
         self.l1 = self.send(1, 1, 1, 1)
@@ -466,31 +746,121 @@
 
 
 RECTS = (
-    (5, (0, 16), 512, 0, 512, 0),
-    (5, (16, 16), 512, 0, 512, 1),
-    (5, (32, 32), 512, 0, 512, 2),
-    (4, (0, 16), 2048, 0, 512, 0),
-    (4, (0, 16), 2048, 512, 1024, 1),
-    (4, (0, 16), 2048, 1536, 512, 2),
-    (3, (0, 16), 512, 0, 512, 0),
-    (0, (0, 16), 512, 0, 512, 0),
-    (1, (0, 16), 512, 0, 512, 1),
-    (2, (0, 16), 512, 0, 512, 2),
+    (5, (0, 16), (0, 512), 0),
+    (5, (16, 16), (0, 512), 1),
+    (5, (32, 32), (0, 512), 2),
+    (4, (0, 16), (0, 512), 0),
+    (4, (0, 16), (512, 1024), 1),
+    (4, (0, 16), (1536, 512), 2),
+    (3, (0, 16), (0, 512), 0),
+    (0, (0, 16), (0, 512), 0),
+    (1, (0, 16), (0, 512), 1),
+    (2, (0, 16), (0, 512), 2),
 )
 BIG_FIRST = tuple(tuple(reversed(o)) for o in ORDER)
 
 
 def reduce_buffers():
     shapes = []
-    for _, (_, rows), _, _, width, order in RECTS:
+    for _, (_, rows), (_, width), order in RECTS:
         a, b, e = BIG_FIRST[order]
         shapes += [
-            CHIPS + (rows, width),
             (3,) + chip_shape((a,)) + (rows, width),
             (3,) + chip_shape((a, b)) + (rows, width),
             (3, rows, width),
         ]
     return shapes
+
+
+class VectorSum:
+    def __init__(self, net, total, bufs):
+        self.net, self.total = net, total
+        self.sib, self.whole, self.vx, self.half, self.vy, self.one, self.vz = bufs
+
+    def start(self):
+        self.c = [self.net.copy(self.total, self.sib, self.net.ring("c", 0))]
+
+    def wait(self):
+        for moved in self.c:
+            moved.wait_recv()
+
+    def along_x(self):
+        self.wait()
+        self.whole[...] = self.total[...] + self.sib[...]
+        self.c = []
+        for k, d in enumerate((1, 3, 2)):
+            x = self.net.moved("x", d)["x"]
+            self.c.append(self.net.copy(self.whole.at[:, columns(256 * x, 256)], self.vx.at[k], self.net.ring("x", d)))
+
+    def along_y(self):
+        self.wait()
+        mine = self.whole[:, columns(256 * self.net.me["x"], 256)]
+        for k in range(3):
+            mine = mine + self.vx[k]
+        self.half[0], self.half[1] = mine[:, :128], mine[:, 128:]
+        self.c = []
+        for k, d in enumerate((1, 3, 2)):
+            lo = lax.rem(self.net.moved("y", d)["y"], 2)
+            self.c.append(self.net.copy(self.half.at[lo], self.vy.at[k], self.net.ring("y", d)))
+
+    def along_z(self):
+        self.wait()
+        mine = self.half[lax.rem(self.net.me["y"], 2)]
+        for k in range(3):
+            mine = mine + self.vy[k]
+        self.one[...] = mine
+        self.c = [self.net.copy(self.one, self.vz.at[k], self.net.ring("z", d)) for k, d in enumerate((1, 3, 2))]
+
+    def done(self, out):
+        self.wait()
+        t = (self.one[...] + self.vz[0]) + (self.vz[1] + self.vz[2])
+        sh = lax.axis_index("shard")
+        to = lax.broadcasted_iota(jnp.int32, (128, 128), 0)
+        i = lax.broadcasted_iota(jnp.int32, (128, 128), 1)
+        place = jnp.where(i < 64, 8 * sh + (i & 7), 32 * lax.rem(sh, 4) + i - 64)
+        pick = jnp.where((place == to) & (i < 96), 1.0, 0.0).astype(BF)
+        high = t.astype(BF)
+        rest = t - high.astype(F32)
+        mid = rest.astype(BF)
+        last = (rest - mid.astype(F32)).astype(BF)
+        got = (mm(high, pick) + mm(mid, pick)) + mm(last, pick)
+        r = lax.broadcasted_iota(jnp.int32, (16, 128), 0)
+        i = lax.broadcasted_iota(jnp.int32, (16, 128), 1)
+        keep = ((i < 64) & (lax.shift_right_logical(i, 3) == r)) | ((i >= 64) & (r == 8 + lax.div(sh, 4)))
+        out[...] = jnp.broadcast_to(jnp.sum(jnp.where(keep, got, 0.0), axis=0, keepdims=True), (8, 128))
+
+
+def attention_back(q, k, v, probs, context, d_context, dq, dk, dv, first, last):
+    def body(h, carry):
+        cols = columns(h * 128, 128)
+        dks, dvs = [], []
+        for b in range(2):
+            mine, near = pl.ds(b * TOK, TOK), pl.ds(b * TOK, SPAN)
+            at = columns((2 * h + b) * OWN, OWN)
+            p = jnp.concatenate([probs[0, :, at], probs[1, :, at]], axis=0)
+            dc = d_context[mine, cols]
+            dc2 = lane_split(dc)
+            prod = (dc.astype(F32) * context[mine, cols].astype(F32)).T
+            dsum = [jnp.sum(prod[s * HEAD : s * HEAD + HEAD], axis=0, keepdims=True) for s in range(2)]
+            dp = mm(v[near, cols], dc2, NT)
+            dr = (p.astype(F32) * ((dp - jnp.concatenate(dsum, axis=1)) * 0.125)).astype(BF)
+            dvs.append(mm(p, dc2))
+            dks.append(mm(dr, lane_split(q[mine, cols])))
+            g = mm(k[near, cols], dr, TN)
+            g = jnp.concatenate([g[:HEAD, :TOK], g[HEAD:, TOK:]], axis=0)
+            dq[mine, cols] = g.T.astype(BF)
+        for d, o in ((dks, dk), (dvs, dv)):
+            o[0:TOK, cols] = d[0][:TOK].astype(BF)
+            o[TOK:SPAN, cols] = (d[0][TOK:] + d[1][: SPAN - TOK]).astype(BF)
+            o[SPAN:WIN, cols] = d[1][SPAN - TOK :].astype(BF)
+        return carry
+
+    lax.fori_loop(first, last, body, 0)
+
+
+def column_sum(x):
+    n, width = x.shape
+    return jnp.sum(jnp.sum(x.astype(F32).reshape(n // 8, 8, width), axis=0), axis=0, keepdims=True)
 
 
 class Return:
@@ -500,18 +870,19 @@
         other = 1 - lo
         self.lo = lo
         self.window, self.back = window, back
-        self.plain = [
-            (window.at[rows_at(HALO + TOK * other, TOK)], back.at[0, lo], net.pair(0, other)),
-            (encoded.at[rows_at(TOK * other, TOK)], out.at[lo], net.pair(0, other)),
-        ]
+        self.plain = [(window.at[rows_at(HALO + TOK * other, TOK)], back.at[0, lo], net.pair(0, other))]
+        self.encoded = (encoded.at[rows_at(TOK * other, TOK)], out.at[lo], net.pair(0, other))
         self.local = pltpu.make_async_copy(encoded.at[rows_at(TOK * lo, TOK)], out.at[lo], local_sem)
         self.base = net.used
         net.used += 16
 
+    def start_encoded(self):
+        self.encoded = self.net.copy(*self.encoded)
+        self.local.start()
+
     def start(self):
         net, lo = self.net, self.lo
-        self.plain = [net.copy(*p) for p in self.plain]
-        self.local.start()
+        self.plain = [net.copy(*p) for p in self.plain] + [self.encoded]
         self.copies = []
         for k in range(4):
             for q in range(2):
@@ -566,206 +937,389 @@
             copy.wait_send()
 
 
-def reduce_kernel(*refs):
-    grads, (window_hbm, encoded) = refs[:6], refs[6:8]
-    outs, out, token_grad = refs[8:14], refs[14], refs[15]
-    rest = refs[16:]
-    full, rest = rest[:6], rest[6:]
-    bufs, rest = rest[:40], rest[40:]
-    window, back = rest[:2]
-    finals, rest = rest[2:8], rest[8:]
-    ends, rest = rest[:6], rest[6:]
-    send_sem, recv_sem, local_sem = rest
-    net = Net(send_sem, recv_sem)
-    c = net.me["c"]
-    loads = [pltpu.make_async_copy(g, f, local_sem.at[k]) for k, (g, f) in enumerate(zip(grads, full))]
-    loads.append(pltpu.make_async_copy(window_hbm, window, local_sem.at[6]))
-    for load in loads:
-        load.start()
-    net.barrier()
-    for load in loads:
-        load.wait()
-    lanes = []
-    for k, (w, (r0, rows), per_core, base, width, order) in enumerate(RECTS):
-        lanes.append(
-            Reduce(
-                net,
-                full[w],
-                pl.ds(r0, rows),
-                c * per_core + base,
-                width,
-                (1 - c) * per_core + base,
-                BIG_FIRST[order],
-                bufs[4 * k : 4 * k + 4],
+class Stream:
+    SLOTS = 4
+
+    def __init__(self, full, ring, sems):
+        wq, wk, wv, wo, wi, wu = full
+        self.ring = ring
+        self.moves = []
+        for n in range(12):
+            slot = ring.at[n % self.SLOTS]
+            if n < 4:
+                pairs = [(wu.at[n], slot)]
+            elif n < 8:
+                pairs = [
+                    (wi.at[n - 4, :, :, :, :, pl.ds(1024 * j, 1024)], slot.at[:, :, :, pl.ds(16 * j, 16)])
+                    for j in range(4)
+                ]
+            else:
+                w = (wo, wk, wv, wq)[n - 8]
+                pairs = [(w.at[x], slot.at[:, :, :, pl.ds(16 * x, 16)]) for x in range(4)]
+            self.moves.append([pltpu.make_async_copy(s, d, sems.at[4 * n + j]) for j, (s, d) in enumerate(pairs)])
+
+    def start(self, n):
+        for move in self.moves[n]:
+            move.start()
+
+    def wait(self, n):
+        for move in self.moves[n]:
+            move.wait()
+
+    def part(self, n, j):
+        return self.ring[n % self.SLOTS, :, :, :, 16 * j : 16 * j + 16].reshape(256, 1024)
+
+
+class Backward:
+    def __init__(self, ins, outs, scratch):
+        self.weights = ins[:6]
+        (self.x_in, self.q_in, self.k_in, self.v_in, self.probs_in, self.context_in, self.low_in, self.act_in) = ins[6:14]
+        (self.slope_in, self.n1_in, self.inv1_in, self.d_in, self.encoded, self.vec, self.two) = ins[14:]
+        self.owned, (self.out, self.token_grad, self.small) = outs[:6], outs[6:]
+        take = iter(scratch)
+        nxt = lambda n: [next(take) for _ in range(n)]
+        (self.ring,) = nxt(1)
+        self.g = nxt(6)
+        self.bufs = nxt(3 * len(RECTS))
+        self.x, self.q, self.k, self.v, self.context, self.low, self.act, self.inner, self.n1, self.inv1, self.d = nxt(11)
+        self.outer, self.outer_sib, self.inner_sib, self.branch, self.branch_sib, self.d_context = nxt(6)
+        self.dq, self.dk, self.dv, self.dq_sib, self.dk_sib, self.dv_sib, self.dx, self.back = nxt(8)
+        self.total, *vector_bufs = nxt(8)
+        self.finals, self.ends = nxt(6), nxt(6)
+        send_sem, recv_sem, self.local_sem = nxt(3)
+        self.net = Net(send_sem, recv_sem)
+        self.c = self.net.me["c"]
+        self.loads = 0
+        self.stream = Stream(self.weights, self.ring, self.local_sem.at[pl.ds(0, 48)])
+        self.vectors = VectorSum(self.net, self.total, vector_bufs)
+        self.back_rows = Return(self.net, self.dx, self.encoded, self.back, self.out, self.local_sem.at[48])
+        lanes = []
+        for n, (w, (r0, rows), (base, width), order) in enumerate(RECTS):
+            lanes.append(
+                Reduce(
+                    self.net,
+                    self.g[w],
+                    pl.ds(r0, rows),
+                    pl.ds(base, width),
+                    BIG_FIRST[order],
+                    self.bufs[3 * n : 3 * n + 3],
+                )
             )
+        self.lanes = {"u": lanes[:3], "i": lanes[3:6], "o": lanes[6:7], "a": lanes[7:]}
+
+    def load(self, src, dst):
+        move = pltpu.make_async_copy(src, dst, self.local_sem.at[49 + self.loads])
+        self.loads += 1
+        move.start()
+        return move
+
+    def half(self, which, width):
+        return columns(which * width, width)
+
+    def share(self, src, dst, width):
+        return self.net.copy(src.at[:, self.half(1 - self.c, width)], dst, self.net.ring("c", 0))
+
+    def begin(self):
+        self.at_d = self.load(self.d_in, self.d)
+        for n in range(4):
+            self.stream.start(n)
+        self.at_slope = self.load(self.slope_in, self.inner)
+        self.at_act = self.load(self.act_in, self.act)
+        self.at_low = self.load(self.low_in, self.low)
+        self.at_n1 = [self.load(self.n1_in, self.n1), self.load(self.inv1_in, self.inv1)]
+        self.at_rest = [
+            self.load(self.context_in, self.context),
+            self.load(self.x_in, self.x),
+            self.load(self.q_in, self.q),
+            self.load(self.k_in, self.k),
+            self.load(self.v_in, self.v),
+        ]
+        self.total[...] = jnp.zeros((16, D), F32)
+        self.total[G2 : G2 + 2, :] = self.two[0:2, :]
+        self.at_d.wait()
+
+        def body(t, carry):
+            r = some_rows(t)
+            low = self.d[r, :].astype(BF)
+            self.outer[r, :] = low
+            return carry + jnp.sum(low.astype(F32).reshape(ROWS // 8, 8, D), axis=0)
+
+        s = lax.fori_loop(0, OWN // ROWS, body, jnp.zeros((8, D), F32))
+        self.total[BU : BU + 1, :] = jnp.sum(s, axis=0, keepdims=True)
+        self.net.barrier()
+        self.got_outer = self.share(self.outer, self.outer_sib, 512)
+        self.back_rows.start_encoded()
+
+    def d_inner(self):
+        self.at_slope.wait()
+        for n in range(4):
+            self.stream.wait(n)
+
+            def body(lo, carry, n=n):
+                at = n * 1024 + lo * 512
+                cols = columns(at, 512)
+                y = mm(self.outer[...], self.ring[n, lo].reshape(512, 1024), NT)
+                y = (y * self.inner[:, cols].astype(F32)).astype(BF)
+                self.inner[:, cols] = y
+                s = column_sum(y)
+                for j in range(4):
+                    dp, t = 2 * n + lo, j
+                    self.total[8 + t : 9 + t, columns(dp * 128, 128)] = s[:, 128 * j : 128 * j + 128]
+                return carry
+
+            lax.fori_loop(0, 2, body, 0)
+            self.stream.start(n + 4)
+        self.got_inner = self.share(self.inner, self.inner_sib, 2048)
+
+    def grad_outer(self):
+        self.at_act.wait()
+        self.got_outer.wait_recv()
+        c = self.c
+        mine = self.outer.at[:, self.half(c, 512)]
+
+        def body(t, carry):
+            cols = columns(t * 512, 512)
+            y = mm(self.act[c, :, cols], mine[...], TN) + mm(self.act[1 - c, :, cols], self.outer_sib[...], TN)
+            self.g[5][lax.div(t, 2), lax.rem(t, 2)] = y.astype(BF).reshape(2, 4, 64, 512)
+            return carry
+
+        lax.fori_loop(0, 8, body, 0)
+        self.at_probs = self.load(self.probs_in, self.act)
+
+    def d_normed(self):
+        for n in range(4):
+            self.stream.wait(4 + n)
+            cols = slice(256 * n, 256 * n + 256)
+            y = self.d[:, cols]
+            for j in range(4):
+                y = y + mm(self.inner[:, 1024 * j : 1024 * j + 1024], self.stream.part(4 + n, j), NT)
+            self.d[:, cols] = y
+            self.stream.start(8 + n)
+
+    def grad_inner(self):
+        self.at_low.wait()
+        self.got_inner.wait_recv()
+        c = self.c
+
+        def body(t, carry):
+            x, j = lax.div(t, 4), lax.rem(t, 4)
+            rows, cols = columns(x * 256, 256), columns(j * 512, 512)
+            y = mm(self.low[c, :, rows], self.inner[:, columns(c * 2048 + j * 512, 512)], TN)
+            y = y + mm(self.low[1 - c, :, rows], self.inner_sib[:, cols], TN)
+            self.g[4][x, :, :, :, :, cols] = y.astype(BF).reshape(2, 2, 4, 16, 512)
+            return carry
+
+        lax.fori_loop(0, 16, body, 0)
+
+    def norm_one(self):
+        for move in self.at_n1:
+            move.wait()
+
+        def body(t, carry):
+            r = some_rows(t)
+            d, n = self.d[r, :], self.n1[r, :]
+            da = norm_back(d * self.vec[G1 : G1 + 1, :], n, self.inv1[r, :1])
+            low = da.astype(BF)
+            self.d[r, :] = da
+            self.branch[r, :] = low
+            new = (d * n, d, low.astype(F32))
+            return tuple(a + jnp.sum(b.reshape(ROWS // 8, 8, D), axis=0) for a, b in zip(carry, new))
+
+        zero = jnp.zeros((8, D), F32)
+        sums = lax.fori_loop(0, OWN // ROWS, body, (zero, zero, zero))
+        for row, s in zip((G1, S1, BO), sums):
+            self.total[row : row + 1, :] = jnp.sum(s, axis=0, keepdims=True)
+        self.got_branch = self.share(self.branch, self.branch_sib, 512)
+
+    def d_mixed(self):
+        self.stream.wait(8)
+        for x in range(4):
+            self.d_context[:, 256 * x : 256 * x + 256] = mm(self.branch[...], self.stream.part(8, x), NT).astype(BF)
+
+    def grad_rows(self, left, right, sib, out):
+        mine = right.at[:, self.half(self.c, 512)]
+
+        def body(x, carry):
+            rows = columns(x * 256, 256)
+            y = mm(left[0][:, rows], mine[...], TN) + mm(left[1][:, rows], sib[...], TN)
+            out[x] = y.astype(BF).reshape(2, 2, 4, 16, 512)
+            return carry
+
+        lax.fori_loop(0, 4, body, 0)
+
+    def pair(self, ref):
+        return ref.at[self.c], ref.at[1 - self.c]
+
+    def grad_output(self):
+        self.got_branch.wait_recv()
+        for move in self.at_rest:
+            move.wait()
+        self.grad_rows(self.pair(self.context), self.branch, self.branch_sib, self.g[3])
+
+    def attend(self, first, last):
+        if first == 0:
+            self.at_probs.wait()
+        attention_back(
+            self.q,
+            self.k,
+            self.v,
+            self.act,
+            self.context.at[self.c],
+            self.d_context,
+            self.dq,
+            self.dk,
+            self.dv,
+            first,
+            last,
         )
-    each(lanes, "d0")
-    back_rows = Return(net, window, encoded, back, out, local_sem.at[7])
-    back_rows.start()
-    first, second, third = lanes[:3], lanes[3:6], lanes[6:]
-    each(first, "p1")
-    each(second, "p1")
-    each(first, "p1_mid")
-    each(third, "p1")
-    each(first, "p2")
-    each(second, "p1_mid")
-    each(first, "p3")
-    each(third, "p1_mid")
-    each(second, "p2")
-    each(third, "p2")
-    each(second, "p3")
-    each(third, "p3")
-    for lane, (w, (r0, rows), per_core, base, width, _) in zip(lanes, RECTS):
-        finals[w][pl.ds(r0, rows), pl.ds(base, width)] = lane.result()
-    swaps = []
-    for w in range(6):
-        n = finals[w].shape[0] // 2
-        width = finals[w].shape[1]
-        kept = finals[w].at[pl.ds(pl.multiple_of(n * c, 8), n)]
-        given = finals[w].at[pl.ds(pl.multiple_of(n * (1 - c), 8), n)]
-        swaps.append(net.copy(given, ends[w].at[:, columns(c * width, width)], net.ring("c", 0)))
-        ends[w][:, columns(c * width, width)] = kept[...]
-    back_rows.gets()
-    back_rows.total(token_grad)
-    for swap in swaps:
-        swap.wait_recv()
-    stores = [pltpu.make_async_copy(e, o, local_sem.at[k]) for k, (e, o) in enumerate(zip(ends, outs))]
-    for store in stores:
-        store.start()
-    for store in stores:
-        store.wait()
-    back_rows.finish()
-    net.finish()
-
-
-def reduce_all(grads, window, encoded):
+
+    def share_heads(self):
+        self.got_heads = [
+            self.share(self.dk, self.dk_sib, 512),
+            self.share(self.dv, self.dv_sib, 512),
+            self.share(self.dq, self.dq_sib, 512),
+        ]
+        self.total[BQ : BQ + 1, :] = column_sum(self.dq[...])
+        self.total[BV : BV + 1, :] = column_sum(self.dv[...])
+        self.vectors.start()
+
+    def grad_key(self):
+        self.got_heads[0].wait_recv()
+        self.grad_rows(self.pair(self.x), self.dk, self.dk_sib, self.g[1])
+
+    def grad_value(self):
+        self.got_heads[1].wait_recv()
+        self.grad_rows(self.pair(self.x), self.dv, self.dv_sib, self.g[2])
+
+    def grad_query(self):
+        self.got_heads[2].wait_recv()
+        own = pl.ds(HALO, OWN)
+        rows = (self.x.at[self.c, own], self.x.at[1 - self.c, own])
+        self.grad_rows(rows, self.dq, self.dq_sib, self.g[0])
+
+    def d_tokens(self):
+        for n in (9, 10, 11):
+            self.stream.wait(n)
+        for x in range(4):
+            cols = slice(256 * x, 256 * x + 256)
+            y = mm(self.dk[...], self.stream.part(9, x), NT) + mm(self.dv[...], self.stream.part(10, x), NT)
+            own = self.d[:, cols] + mm(self.dq[...], self.stream.part(11, x), NT)
+            self.dx[:HALO, cols] = y[:HALO].astype(BF)
+            self.dx[HALO : HALO + OWN, cols] = (y[HALO : HALO + OWN] + own).astype(BF)
+            self.dx[HALO + OWN :, cols] = y[HALO + OWN :].astype(BF)
+        self.back_rows.start()
+
+    def finish(self):
+        c, net = self.c, self.net
+        done = [lane for group in ("u", "i", "o", "a") for lane in self.lanes[group]]
+        swaps = []
+        rects = list(zip(done, RECTS))
+        for w in (5, 4, 3, 0, 1, 2):
+            final, end = self.finals[w], self.ends[w]
+            for lane, (of, (r0, rows), (base, width), _) in rects:
+                if of == w:
+                    final[pl.ds(r0, rows), pl.ds(base, width)] = lane.result()
+            n, width = final.shape[0] // 2, final.shape[1]
+            kept = final.at[pl.ds(pl.multiple_of(n * c, 8), n)]
+            given = final.at[pl.ds(pl.multiple_of(n * (1 - c), 8), n)]
+            swaps.append((w, net.copy(given, end.at[:, columns(c * width, width)], net.ring("c", 0))))
+            end[:, columns(c * width, width)] = kept[...]
+        self.back_rows.gets()
+        self.back_rows.total(self.token_grad)
+        self.vectors.done(self.small)
+        stores = []
+        for w, swap in swaps:
+            swap.wait_recv()
+            stores.append(self.load(self.ends[w], self.owned[w]))
+        for store in stores:
+            store.wait()
+        self.back_rows.finish()
+        net.finish()
+
+
+BACK = (
+    "begin", "d_inner", "grad_outer", "u.p1", "d_normed", "u.p1_mid", "grad_inner", "i.p1", "norm_one",
+    "d_mixed", "u.p2", "i.p1_mid", "grad_output", "o.p1", "attend.0.3", "u.p3", "i.p2", "attend.3.6",
+    "o.p1_mid", "i.p3", "attend.6.8", "share_heads", "d_tokens", "grad_key", "grad_value", "grad_query",
+    "a.p1", "vectors.along_x", "o.p2", "vectors.along_y", "a.p1_mid", "o.p3", "vectors.along_z", "a.p2",
+    "a.p3", "finish",
+)
+
+
+def run_steps(work, steps):
+    for step in steps:
+        name, *rest = step.split(".")
+        if name in work.lanes:
+            each(work.lanes[name], rest[0])
+        elif name == "vectors":
+            getattr(work.vectors, rest[0])()
+        else:
+            getattr(work, name)(*map(int, rest))
+
+
+def backward_kernel(*refs):
+    run_steps(Backward(refs[:21], refs[21:30], refs[30:]), BACK)
+
+
+def backward_all(kept):
     any_space = pl.BlockSpec(memory_space=pl.ANY)
-    full = [CHIPS + s for s in BLOCKS]
+    vmem = pl.BlockSpec(memory_space=pltpu.VMEM)
     owned = [(r // 2, n) for r, n in BLOCKS]
+    scratch = [((4, 2, 2, 4, 64, 1024), BF)]
+    scratch += [(CHIPS + (r, n // 2), BF) for r, n in BLOCKS]
+    scratch += [(s, BF) for s in reduce_buffers()]
+    scratch += [((2, WIN, D), BF), ((OWN, D), BF), ((WIN, D), BF), ((WIN, D), BF), ((2, OWN, D), BF), ((2, OWN, D), BF)]
+    scratch += [((2, OWN, FF), BF), ((OWN, FF), BF), ((OWN, D), F32), ((OWN, 128), F32), ((OWN, D), F32)]
+    scratch += [((OWN, D), BF), ((OWN, 512), BF), ((OWN, 2048), BF), ((OWN, D), BF), ((OWN, 512), BF), ((OWN, D), BF)]
+    scratch += [((OWN, D), BF), ((WIN, D), BF), ((WIN, D), BF), ((OWN, 512), BF), ((WIN, 512), BF), ((WIN, 512), BF)]
+    scratch += [((WIN, D), BF), ((3, 2, TOK, D), BF)]
+    scratch += [((16, D), F32), ((16, D), F32), ((16, D), F32), ((3, 16, 256), F32), ((2, 16, 128), F32), ((3, 16, 128), F32)]
+    scratch += [((16, 128), F32), ((3, 16, 128), F32)]
+    scratch += [((r, n // 2), F32) for r, n in BLOCKS] + [(s, F32) for s in owned]
     return pl.pallas_call(
-        reduce_kernel,
-        name="reduce_all",
+        backward_kernel,
+        name="backward_all",
         out_shape=[jax.ShapeDtypeStruct(s, F32) for s in owned]
-        + [jax.ShapeDtypeStruct((2, TOK, D), BF), jax.ShapeDtypeStruct((2, TOK, D), BF)],
-        in_specs=[any_space] * 8,
-        out_specs=[any_space] * 7 + [pl.BlockSpec(memory_space=pltpu.VMEM)],
-        scratch_shapes=[pltpu.VMEM(s, BF) for s in full]
-        + [pltpu.VMEM(s, BF) for s in reduce_buffers()]
-        + [pltpu.VMEM((WIN, D), BF), pltpu.VMEM((3, 2, TOK, D), BF)]
-        + [pltpu.VMEM((r, n // 2), F32) for r, n in BLOCKS]
-        + [pltpu.VMEM(s, F32) for s in owned]
+        + [jax.ShapeDtypeStruct((2, TOK, D), BF)] * 2
+        + [jax.ShapeDtypeStruct((8, 128), F32)],
+        in_specs=[any_space] * 19 + [vmem] * 2,
+        out_specs=[any_space] * 7 + [vmem] * 2,
+        scratch_shapes=[pltpu.VMEM(s, t) for s, t in scratch]
         + [
             pltpu.SemaphoreType.DMA((N_SEM,)),
             pltpu.SemaphoreType.DMA((N_SEM,)),
-            pltpu.SemaphoreType.DMA((8,)),
+            pltpu.SemaphoreType.DMA((80,)),
         ],
-        compiler_params=pltpu.CompilerParams(collective_id=2, has_side_effects=True, vmem_limit_bytes=62 << 20),
-    )(*grads, window, encoded)
-
-
-def dot(a, b):
-    return jnp.dot(a, b, preferred_element_type=F32)
-
-
-def norm(a, gain, shift):
-    centred = a - jnp.mean(a, axis=-1, keepdims=True)
-    inv = lax.rsqrt(jnp.mean(centred * centred, axis=-1, keepdims=True) + 1e-05)
-    n = centred * inv
-    return n * gain + shift, n, inv
-
-
-def norm_back(d, n, inv, gain):
-    dn = d * gain
-    da = inv * (dn - jnp.mean(dn, axis=-1, keepdims=True) - n * jnp.mean(dn * n, axis=-1, keepdims=True))
-    return da, jnp.sum(d * n, axis=0), jnp.sum(d, axis=0)
-
-
-def segments(lengths, order, start, count):
-    ends = jnp.cumsum(jnp.take(lengths, order))
-    at = start + jnp.arange(count)
-    segment = jnp.sum((ends[:, None] <= at[None, :]).astype(jnp.int32), axis=0)
-    return jnp.where(at < 0, -1, segment)
-
-
-def layer(window, cots, segment, full, vectors):
-    wq, wk, wv, wo, wi, wu = full
-    bq, bv, bo, g1, s1, bu, g2, s2, bi = [v.astype(F32) for v in vectors]
-    rows = window[HALO : HALO + OWN]
-    q = (dot(rows, wq) + bq).astype(BF).reshape(OWN, HEADS, HEAD)
-    k = dot(window, wk).astype(BF).reshape(WIN, HEADS, HEAD)
-    v = (dot(window, wv) + bv).astype(BF).reshape(WIN, HEADS, HEAD)
-    same = (segment[HALO : HALO + OWN, None] == segment[None, :])[None]
-    scores = jnp.einsum("qhd,khd->hqk", q, k, preferred_element_type=F32) * 0.125
-    scores = jnp.where(same, scores, -1e30)
-    e = jnp.exp(scores - jnp.max(scores, axis=-1, keepdims=True))
-    probs = e / jnp.sum(e, axis=-1, keepdims=True)
-    low = probs.astype(BF)
-    mixed = jnp.einsum("hqk,khd->qhd", low, v, preferred_element_type=F32)
-    context = mixed.reshape(OWN, D).astype(BF)
-    attended = rows.astype(F32) + (dot(context, wo) + bo)
-    normed, n1, inv1 = norm(attended, g1, s1)
-    normed_low = normed.astype(BF)
-    pre = dot(normed_low, wi) + bi
-    phi = 0.5 * (1.0 + lax.erf(pre * math.sqrt(0.5)))
-    activated = (pre * phi).astype(BF)
-    slope = phi + pre * jnp.exp(-0.5 * pre * pre) * (1.0 / math.sqrt(2 * math.pi))
-    encoded, n2, inv2 = norm(normed + (dot(activated, wu) + bu), g2, s2)
-    d_final, dg2, ds2 = norm_back(cots.astype(F32), n2, inv2, g2)
-    d_outer = d_final.astype(BF)
-    tdot = lambda a, b: lax.dot_general(a, b, (((0,), (0,)), ((), ())), preferred_element_type=F32)
-    dott = lambda a, b: lax.dot_general(a, b, (((1,), (1,)), ((), ())), preferred_element_type=F32)
-    gwu = tdot(activated, d_outer).astype(BF)
-    dbu = jnp.sum(d_outer.astype(F32), axis=0)
-    d_inner = (dott(d_outer, wu) * slope).astype(BF)
-    gwi = tdot(normed_low, d_inner).astype(BF)
-    dbi = jnp.sum(d_inner.astype(F32), axis=0)
-    d_normed = d_final + dott(d_inner, wi)
-    d_attended, dg1, ds1 = norm_back(d_normed, n1, inv1, g1)
-    d_branch = d_attended.astype(BF)
-    gwo = tdot(context, d_branch).astype(BF)
-    dbo = jnp.sum(d_branch.astype(F32), axis=0)
-    d_context = dott(d_branch, wo).astype(BF)
-    dc = d_context.reshape(OWN, HEADS, HEAD)
-    dv = jnp.einsum("hqk,qhd->khd", low, dc, preferred_element_type=F32).reshape(WIN, D).astype(BF)
-    dp = jnp.einsum("qhd,khd->hqk", dc, v, preferred_element_type=F32)
-    dsum = jnp.sum((d_context.astype(F32) * context.astype(F32)).reshape(OWN, HEADS, HEAD), axis=-1)
-    dr = (probs * (dp - dsum.T[:, :, None]) * 0.125).astype(BF)
-    dq = jnp.einsum("hqk,khd->qhd", dr, k, preferred_element_type=F32).reshape(OWN, D).astype(BF)
-    dk = jnp.einsum("hqk,qhd->khd", dr, q, preferred_element_type=F32).reshape(WIN, D).astype(BF)
-    gwq = tdot(rows, dq).astype(BF)
-    gwk = tdot(window, dk).astype(BF)
-    gwv = tdot(window, dv).astype(BF)
-    dbq = jnp.sum(dq.astype(F32), axis=0)
-    dbv = jnp.sum(dv.astype(F32), axis=0)
-    dx = dott(dk, wk) + dott(dv, wv)
-    mid = dx[HALO : HALO + OWN] + d_attended + dott(dq, wq)
-    dx = jnp.concatenate([dx[:HALO], mid, dx[HALO + OWN :]], axis=0).astype(BF)
-    grads = (gwq, gwk, gwv, gwo, gwi, gwu)
-    return encoded.astype(BF), dx, grads, (dbq, dbv, dbo, dg1, ds1, dbu, dg2, ds2, dbi)
+        compiler_params=pltpu.CompilerParams(collective_id=2, has_side_effects=True, vmem_limit_bytes=63 << 20),
+    )(*kept)
 
 
 def local(
     tokens, cotangent, seq_lengths, block_offsets, deal_order, wq, wk, wv, wo, bq, bv, bo, g1, s1, wi, bi, wu, bu, g2, s2
 ):
-    lo = lax.rem(lax.axis_index("dp"), 2)
-    own = jnp.concatenate([wq, wk, wv, wo] + [wi[:, D * j : D * j + D] for j in range(4)] + [wu], axis=0)
-    gathered = gather_all(own, tokens[:, 0], cotangent[:, 0])
-    full = [w.reshape(-1, w.shape[-1]) for w in gathered[:6]]
-    window, cots = gathered[6:]
-    small = jnp.concatenate([bq, bv, bo, g1, s1, bu, g2, s2, bi])
-    both = lax.all_gather(small, ("dp", "shard"), axis=0)
-    vectors = [both[:, 8 * j : 8 * j + 8].reshape(-1) for j in range(8)] + [both[:, 64:].reshape(-1)]
-    lengths = lax.dynamic_index_in_dim(seq_lengths[:, 0], lo, 0, keepdims=False)
-    order = lax.dynamic_index_in_dim(deal_order[:, 0], lo, 0, keepdims=False)
-    start = lax.div(lax.axis_index("dp"), 2) * OWN - HALO
-    segment = segments(lengths, order, start, WIN)
-    encoded, dx, grads, small_grads = layer(window, cots, segment, full, vectors)
-    blocked = [g.reshape(CHIPS + s) for g, s in zip(grads, BLOCKS)]
-    *owned, out, token_grad = reduce_all(blocked, dx, encoded)
-    lines = jnp.concatenate([g.reshape(128, -1) for g in small_grads], axis=1)
-    mine = lax.psum_scatter(lines, ("dp", "shard"), scatter_dimension=0, tiled=True)[0]
+    small = jnp.pad(jnp.concatenate([bq, bv, bo, g1, s1, bu, g2, s2, bi]), (0, 32))[None]
+    kept = forward_all(
+        tokens[:, 0], cotangent[:, 0], seq_lengths[:, 0], deal_order[:, 0], small, (wq, wk, wv, wo, wi, wu)
+    )
+    *owned, out, token_grad, sums = backward_all(kept)
+    mine = sums[0]
     sbq, sbv, sbo, sg1, ss1, sbu, sg2, ss2 = [mine[8 * j : 8 * j + 8] for j in range(8)]
-    return (out[:, None], token_grad[:, None], *owned[:4], sbq, sbv, sbo, sg1, ss1, owned[4], mine[64:], owned[5], sbu, sg2, ss2)
+    return (
+        out[:, None],
+        token_grad[:, None],
+        *owned[:4],
+        sbq,
+        sbv,
+        sbo,
+        sg1,
+        ss1,
+        owned[4],
+        mine[64:96],
+        owned[5],
+        sbu,
+        sg2,
+        ss2,
+    )
 
 
 def solution(mesh):

time: 491 us -> 226 us (0.46)
  blocking collectives: 128 us -> 0 us
  matrix products: 99.9 us -> 0 us
  local copies, waits for them, and re-layouts: 55.2 us -> 17 us
  Pallas kernels: 184 us -> 207 us
  other arithmetic: 17.6 us -> 0 us
    unnamed x2 -> x0, blocking collectives: 128 us -> none
    dot_general x23 -> x0, matrix products: 90.8 us -> none  [the longest x6 29 us: dot(): return jnp.dot(a, b, preferred_element_type=F32)]
    pallas_call x2, Pallas kernels: 184 us -> 207 us  [the longest x1 107 us: backward_all(): pl.pallas_call(backward_kernel, name='backward_all', out_shape=[jax.Shape...]
    unnamed x75 -> x20, local copies, waits for them, and re-layouts: 22.2 us -> 7.53 us
    convert_element_type x14 -> x0, local copies, waits for them, and re-layouts: 11.7 us -> none  [the longest x9 2.48 us: layer(): bq, bv, bo, g1, s1, bu, g2, s2, bi = [v.astype(F32) for v in vectors]]
    sub x1 -> x0, matrix products: 9.16 us -> none  [layer(): e = jnp.exp(scores - jnp.max(scores, axis=-1, keepdims=True))]
    convert_element_type x3 -> x0, other arithmetic: 8.2 us -> none  [the longest x1 7.3 us: layer(): low = probs.astype(BF)]
    reshape x9 -> x0, local copies, waits for them, and re-layouts: 7.85 us -> none  [local(): lines = jnp.concatenate([g.reshape(128, -1) for g in small_grads], axis=1)]
where the time goes in v2:
time: 226 us; the launch traced here: 225 us
  Pallas kernels  207 us (92%)
  local copies, waits for them, and re-layouts  17 us (8%)
    pallas_call x1, Pallas kernels, backward_all(): pl.pallas_call(backward_kernel, name='backward_all', out_shape=[jax.Shape...  107 us
    pallas_call x1, Pallas kernels, forward_all(): pl.pallas_call(forward_kernel, name='forward_all', out_shape=[jax.ShapeDt...  100 us
    unnamed x20, local copies, waits for them, and re-layouts  7.53 us
    concatenate x1, local copies, waits for them, and re-layouts, local(): jnp.concatenate([bq, bv, bo, g1, s1, bu, g2, s2, bi])  6.1 us

profile of v2, /device:TPU:1, one launch (start us, length us, event | category | flops | bytes accessed | tf_op | source)
XLA Modules:
  0.0 225.2 jit_solution(12325253118397217856)
XLA Ops:
  0.7 6.1 %concatenate.3 = bf16[96]{0:T(256)(128)(2,1)S(1)} concatenate(bf16[8]{0:T(256)(128)(2,1)} %param.28, bf16[8]{0:T(256)(128)(2,1)} %param.29, bf16[8]{0:T(256)(128)(2,1)} %param.30, bf16[8]{0:T(256)(128)(2,1)} %param.31, bf16[8]{0:T(256)(128)(2,1)} %param.32, bf16[8]{0:T(256)(128)(2,1)} %param.36, bf16[8]{0:T(256)(128)(2,1)} %param.37, bf16[8]{0:T(256)(128)(2,1)} %param.38, ...), dimensions={0} | concatenate | bytes 384 | tf_op jit(solution)/shard_map/concatenate | solution.py:1300
  6.8 0.5 pad_bitcast_fusion.refs_4_
  7.3 100.2 %forward_all.1 = (bf16[4,2,2,4,16,1024]{5,4,3,2,1,0:T(8,128)(2,1)}, bf16[4,2,2,4,16,1024]{5,4,3,2,1,0:T(8,128)(2,1)}, bf16[4,2,2,4,16,1024]{5,4,3,2,1,0:T(8,128)...) custom-call(bf16[2,128,1024]{2,1,0:T(8,128)(2,1)} %bitcast.30, ...), custom_call_target="tpu_custom_call" | custom-call | tf_op jit(solution)/shard_map/forward_all/pallas_call | solution.py:648
  107.5 107.3 %backward_all.1 = (f32[8,1024]{1,0:T(8,128)}, f32[8,1024]{1,0:T(8,128)}, f32[8,1024]{1,0:T(8,128)}, f32[8,1024]{1,0:T(8,128)}, f32[8,4096]{1,0:T(8,128)}, /*inde...) custom-call(bf16[4,2,2,4,16,1024]{5,4,3,2,1,0:T(8,128)(2,1)} %get-tuple-element., ...), custom_call_target="tpu_custom_call" | custom-call | tf_op jit(solution)/shard_map/backward_all/pallas_call | solution.py:1279
  214.8 0.0 copy-start.5
  214.8 0.0 copy-start.4
  214.8 0.0 copy-start.3
  214.8 0.0 copy-start.2
  214.8 0.0 copy-start.1
  214.8 0.0 copy-start
  214.8 1.3 slice_bitcast_fusion.3
  216.2 1.6 slice_bitcast_fusion
  217.7 1.9 copy.46
  219.6 1.9 copy.47
  221.5 0.0 copy-done.5
  221.5 0.6 copy.48
  222.1 0.0 copy-done.4
  222.1 0.6 copy.49
  222.7 0.0 copy-done.3
  222.7 0.6 copy.50
  223.3 0.0 copy-done.2
  223.3 0.6 copy.51
  223.9 0.7 copy.52
  224.6 0.7 copy.53
  (2 shorter events, 0.0 us)
Async XLA Ops:
  214.8 6.7 %copy-start.5 = (f32[8,1024]{1,0:T(8,128)S(1)}, f32[8,1024]{1,0:T(8,128)}, u32[]{:S(2)}) copy-start(f32[8,1024]{1,0:T(8,128)} %get-tuple-element.121) | copy-start | bytes 98308
  214.8 7.3 %copy-start.4 = (f32[8,1024]{1,0:T(8,128)S(1)}, f32[8,1024]{1,0:T(8,128)}, u32[]{:S(2)}) copy-start(f32[8,1024]{1,0:T(8,128)} %get-tuple-element.122) | copy-start | bytes 98308
  214.8 7.9 %copy-start.3 = (f32[8,1024]{1,0:T(8,128)S(1)}, f32[8,1024]{1,0:T(8,128)}, u32[]{:S(2)}) copy-start(f32[8,1024]{1,0:T(8,128)} %get-tuple-element.123) | copy-start | bytes 98308
  214.8 8.5 %copy-start.2 = (f32[8,1024]{1,0:T(8,128)S(1)}, f32[8,1024]{1,0:T(8,128)}, u32[]{:S(2)}) copy-start(f32[8,1024]{1,0:T(8,128)} %get-tuple-element.124) | copy-start | bytes 98308
  214.8 9.1 %copy-start.1 = (f32[8,4096]{1,0:T(8,128)S(1)}, f32[8,4096]{1,0:T(8,128)}, u32[]{:S(2)}) copy-start(f32[8,4096]{1,0:T(8,128)} %get-tuple-element.130) | copy-start | bytes 393220
  214.8 9.8 %copy-start = (f32[32,1024]{1,0:T(8,128)S(1)}, f32[32,1024]{1,0:T(8,128)}, u32[]{:S(2)}) copy-start(f32[32,1024]{1,0:T(8,128)} %get-tuple-element.132) | copy-start | bytes 393220

commit v3 on v2

--- a/solution.py
+++ b/solution.py
@@ -59,40 +59,32 @@
     def ring(self, axis, by):
         return device_at(self.moved(axis, by))
 
-    def pair(self, by, lo):
-        at = self.moved("x", by % 4)
+    def pair(self, lo):
+        at = dict(self.me)
         at["y"] = lax.div(at["y"], 2) * 2 + lo
         return device_at(at)
 
-    def slot(self):
+    def copy(self, src, dst, device):
+        k = self.used
         self.used += 1
-        return self.used - 1
-
-    def make(self, src, dst, device, send, recv):
-        return pltpu.make_async_remote_copy(
+        moved = pltpu.make_async_remote_copy(
             src_ref=src,
             dst_ref=dst,
-            send_sem=self.send_sem.at[send],
-            recv_sem=self.recv_sem.at[recv],
+            send_sem=self.send_sem.at[k],
+            recv_sem=self.recv_sem.at[k],
             device_id=device,
             device_id_type=MESH,
         )
-
-    def copy(self, src, dst, device):
-        k = self.slot()
-        moved = self.make(src, dst, device, k, k)
         moved.start()
         self.sent.append(moved)
         return moved
 
-    def barrier(self):
+    def greet(self):
         bar = pltpu.get_barrier_semaphore()
         peers = [self.ring("c", 0)] + [self.ring(a, b) for a in AXES for b in (1, 2, 3)]
-        other = 1 - lax.rem(self.me["y"], 2)
-        peers += [self.pair(1, other), self.pair(3, other)]
         for p in peers:
             pl.semaphore_signal(bar, inc=1, device_id=p, device_id_type=MESH)
-        pl.semaphore_wait(bar, len(peers))
+        return lambda: pl.semaphore_wait(bar, len(peers))
 
     def finish(self):
         for moved in self.sent:
@@ -155,6 +147,18 @@
             moved.wait_recv()
         self.c = [self.send(self.at(**{self.a: None}), self.b, d) for d in (1, 3, 2)]
 
+    def p2_ring(self):
+        for moved in self.c:
+            moved.wait_recv()
+        self.c = [self.send(self.at(**{self.a: None}), self.b, d) for d in (1, 3)]
+
+    def p2_mid(self):
+        for h, (moved, to) in enumerate(zip(self.c, (1, 3))):
+            moved.wait_recv()
+            b = self.net.moved(self.b, 4 - to)[self.b]
+            self.c.append(self.send(self.at(**{self.a: ("half", h), self.b: b}), self.b, to))
+        self.c = self.c[2:]
+
     def part(self, h, by):
         e = self.net.moved(self.e, by)[self.e]
         return self.at(**{self.a: h if h is None else ("half", h), self.b: None, self.e: e})
@@ -195,79 +199,47 @@
         getattr(lane, step)()
 
 
-def pieces(lo):
-    at = TOK * lo
-    return (
-        (1, pl.ds(TOK // 2, TOK // 2), at + TOK // 2 - (OWN - HALO), None),
-        (1, pl.ds(0, TOK // 2), at - (OWN - HALO), 1),
-        (-1, pl.ds(0, TOK // 2), at + HALO + OWN, None),
-        (-1, pl.ds(TOK // 2, TOK // 2), at + TOK // 2 + HALO + OWN, 0),
-    )
-
-
 def rows_at(base, count):
     return pl.ds(pl.multiple_of(base, TOK // 2), count)
 
 
 class Window:
     def __init__(self, net, tokens, cotangent, window, cots, local_sem):
-        self.net = net
-        lo = lax.rem(net.me["y"], 2)
-        other = 1 - lo
-        self.copies = []
-        mine = rows_at(HALO + TOK * lo, TOK)
-        theirs = rows_at(TOK * lo, TOK)
-        self.local = [
-            pltpu.make_async_copy(tokens.at[lo], window.at[mine], local_sem.at[0]),
-            pltpu.make_async_copy(cotangent.at[lo], cots.at[theirs], local_sem.at[1]),
+        self.net, self.window, self.cots = net, window, cots
+        self.tokens, self.cotangent, self.local_sem = tokens, cotangent, local_sem
+        self.lo = lax.rem(net.me["y"], 2)
+
+    def pair(self, src, dst, sem):
+        local = pltpu.make_async_copy(src.at[self.lo], dst, sem)
+        local.start()
+        return local, self.net.copy(src.at[1 - self.lo], dst, self.net.pair(1 - self.lo))
+
+    def start(self):
+        mine = self.window.at[rows_at(HALO + TOK * self.lo, TOK)]
+        self.rows = self.pair(self.tokens, mine, self.local_sem.at[0])
+
+    def start_cots(self):
+        mine = self.cots.at[rows_at(TOK * self.lo, TOK)]
+        self.cot_rows = self.pair(self.cotangent, mine, self.local_sem.at[1])
+
+    def halo(self):
+        local, moved = self.rows
+        local.wait()
+        moved.wait_recv()
+        w, net = self.window, self.net
+        self.c = [
+            net.copy(w.at[pl.ds(OWN, HALO)], w.at[pl.ds(0, HALO)], net.ring("x", 1)),
+            net.copy(w.at[pl.ds(HALO, HALO)], w.at[pl.ds(HALO + OWN, HALO)], net.ring("x", 3)),
         ]
-        self.pair = [
-            (tokens.at[other], window.at[mine]),
-            (cotangent.at[other], cots.at[theirs]),
-        ]
-        self.halo = []
-        for by, rows, to, only in pieces(lo):
-            first = net.slot()
-            second = net.slot()
-            for m in range(2):
-                send = first if m == 0 else second
-                copy = net.make(
-                    tokens.at[m, rows], window.at[rows_at(to, TOK // 2)], net.pair(by, m), send, first + lo
-                )
-                self.halo.append((copy, only))
-        self.gets = []
-        for k, (by, rows, to, only) in enumerate(pieces(lo)):
-            for source in range(2):
-                if only is None or only == source:
-                    index = 2 * k + source + (net.used - 8)
-                    self.gets.append(
-                        net.make(tokens.at[0, rows], window.at[pl.ds(0, TOK // 2)], net.pair(1, other), 0, index)
-                    )
-
-    def start(self):
-        for copy in self.local:
-            copy.start()
-        lo = lax.rem(self.net.me["y"], 2)
-        self.pair = [self.net.copy(s, d, self.net.pair(0, 1 - lo)) for s, d in self.pair]
-        for copy, only in self.halo:
-            if only is None:
-                copy.start()
-            else:
-                pl.when(lo == only)(copy.start)
 
     def done(self):
-        for copy in self.local:
-            copy.wait()
-        for copy in self.pair + self.gets:
-            copy.wait_recv()
-
-    def finish(self):
-        lo = lax.rem(self.net.me["y"], 2)
-        for copy, only in self.halo:
-            if only is None:
-                copy.wait_send()
-            else:
-                pl.when(lo == only)(copy.wait_send)
+        for moved in self.c:
+            moved.wait_recv()
+
+    def cots_done(self):
+        local, moved = self.cot_rows
+        local.wait()
+        moved.wait_recv()
 
 
 def place_own(me, mine, peer, full):
@@ -399,8 +371,8 @@
 
 
 class Vectors:
-    def __init__(self, net, small, tiles, vec, inner):
-        self.net, self.small = net, small
+    def __init__(self, net, small, rows, tiles, vec, inner):
+        self.net, self.small, self.rows = net, small, rows
         self.own, self.sib, self.tz, self.ty, self.tx = tiles
         self.vec, self.inner = vec, inner
 
@@ -409,16 +381,19 @@
 
     def start(self):
         sh = lax.axis_index("shard")
-        r = lax.broadcasted_iota(jnp.int32, (16, 128), 0)
-        i = lax.broadcasted_iota(jnp.int32, (16, 128), 1)
-        value = jnp.broadcast_to(self.small[0:1, :].astype(F32), (16, 128))
-        part = (i < 64) & (lax.shift_right_logical(i, 3) == r)
-        inner = (i >= 64) & (i < 96) & (r == 8 + lax.div(sh, 4))
-        picked = jnp.where(part | inner, value, 0.0).astype(BF)
+        self.rows[...] = jnp.zeros((16, 128), F32)
+        for j in range(9):
+            n = self.small[j].shape[1]
+            self.rows[j : j + 1, :n] = self.small[j][...].astype(F32)
         i = lax.broadcasted_iota(jnp.int32, (128, 128), 0)
         to = lax.broadcasted_iota(jnp.int32, (128, 128), 1)
-        place = jnp.where(i < 64, 8 * sh + (i & 7), 32 * lax.rem(sh, 4) + i - 64)
-        self.own[...] = mm(picked, jnp.where((place == to) & (i < 96), 1.0, 0.0).astype(BF)).astype(BF)
+        value = self.rows[...].astype(BF)
+        eight = mm(value, jnp.where((to == 8 * sh + i) & (i < 8), 1.0, 0.0).astype(BF))
+        many = mm(value, jnp.where((to == 32 * lax.rem(sh, 4) + i) & (i < 32), 1.0, 0.0).astype(BF))
+        r = lax.broadcasted_iota(jnp.int32, (16, 128), 0)
+        many = jnp.broadcast_to(many[8:9], (16, 128))
+        tile = jnp.where(r < 8, eight, jnp.where(r == 8 + lax.div(sh, 4), many, 0.0))
+        self.own[...] = tile.astype(BF)
         self.c = [self.net.copy(self.own, self.sib, self.net.ring("c", 0))]
 
     def wait(self):
@@ -457,167 +432,202 @@
 BQ, BV, BO, G1, S1, BU, G2, S2 = range(8)
 
 
+class Forward:
+    def __init__(self, ins, outs, scratch):
+        self.tokens, self.cotangent, self.lengths, self.order = ins[:4]
+        self.own, self.small = ins[4:10], ins[10:]
+        self.weights_out = outs[:6]
+        (self.x_out, self.q_out, self.k_out, self.v_out, self.probs_out, self.context_out, self.low_out) = outs[6:13]
+        (self.act_out, self.slope_out, self.n1_out, self.inv1_out, self.d_out, self.encoded_out) = outs[13:19]
+        self.vec_out, self.two_out = outs[19:]
+        self.mine, self.peer = scratch[:2]
+        self.full, scratch = scratch[2:8], scratch[8:]
+        (self.window, self.cots, self.q, self.k, self.v, self.probs, self.context, self.low) = scratch[:8]
+        (self.act, self.slope, self.bias, self.n1, self.inv1, self.normed, self.total, self.encoded) = scratch[8:16]
+        self.vec, self.inner, self.two, self.placed = scratch[16:20]
+        tiles, (send_sem, recv_sem, self.local_sem) = scratch[20:25], scratch[25:]
+        self.net = Net(send_sem, recv_sem)
+        self.me, self.c = self.net.me, self.net.me["c"]
+        self.lo = lax.rem(self.me["y"], 2)
+        self.stores, self.gets = [], []
+        self.vectors = Vectors(self.net, self.small, self.placed, tiles, self.vec, self.inner)
+        self.view = Window(self.net, self.tokens, self.cotangent, self.window, self.cots, self.local_sem)
+        rows, half = slice(None), columns(self.c * 512, 512)
+        wi, wu = self.full[4], self.full[5]
+
+        def inner(base, width, order):
+            return Gather(self.net, wi, rows, columns(self.c * 2048 + base, width), ORDER[order])
+
+        self.lanes = {
+            "a": [Gather(self.net, self.full[j], rows, half, ORDER[j]) for j in range(3)],
+            "b": [Gather(self.net, self.full[3], rows, half, ORDER[2]), inner(0, 1024, 1), inner(1024, 1024, 2)],
+            "u": [
+                Gather(self.net, wu, pl.ds(0, 32), half, ORDER[0]),
+                Gather(self.net, wu, pl.ds(32, 16), half, ORDER[1]),
+                Gather(self.net, wu, pl.ds(48, 16), half, ORDER[2]),
+            ],
+        }
+
+    def store(self, src, dst):
+        move = pltpu.make_async_copy(src, dst, self.local_sem.at[2 + len(self.stores)])
+        move.start()
+        self.stores.append(move)
+
+    def both(self, src, dst):
+        self.gets.append(self.net.copy(src, dst.at[self.c], self.net.ring("c", 0)))
+        self.store(src, dst.at[self.c])
+
+    def begin(self):
+        greeted = self.net.greet()
+        for j in range(4):
+            self.mine[8 * j : 8 * j + 8, :] = self.own[j][...]
+            self.mine[32 + 8 * j : 40 + 8 * j, :] = self.own[4][:, 1024 * j : 1024 * j + 1024]
+        self.mine[64:96, :] = self.own[5][...]
+        greeted()
+        swap = self.net.copy(self.mine, self.peer, self.net.ring("c", 0))
+        self.view.start()
+        self.vectors.start()
+        swap.wait_recv()
+        place_own(self.me, self.mine, self.peer, self.full)
+
+    def halo(self):
+        self.view.halo()
+
+    def cots_in(self):
+        self.view.start_cots()
+
+    def masks(self):
+        segment_bias(self.lengths, self.order, self.me["x"] * OWN - HALO, self.lo, self.bias)
+
+    def rows_done(self):
+        self.view.done()
+        self.both(self.window, self.x_out)
+
+    def query(self):
+        project(self.window.at[pl.ds(HALO, OWN)], self.full[0], self.q, self.vec.at[BQ : BQ + 1])
+
+    def key(self):
+        project(self.window, self.full[1], self.k)
+
+    def value(self):
+        project(self.window, self.full[2], self.v, self.vec.at[BV : BV + 1])
+
+    def keep_heads(self):
+        for j in range(3):
+            self.store(self.full[j], self.weights_out[j])
+        for src, dst in ((self.q, self.q_out), (self.k, self.k_out), (self.v, self.v_out)):
+            self.store(src, dst)
+
+    def attend(self, first, last):
+        attention(self.q, self.k, self.v, self.bias, self.probs, self.context, first, last)
+
+    def keep_probs(self):
+        self.both(self.context, self.context_out)
+        self.store(self.probs, self.probs_out)
+
+    def mix(self):
+        self.store(self.full[3], self.weights_out[3])
+        self.store(self.full[4], self.weights_out[4])
+
+        def body(t, carry):
+            cols = columns(t * 512, 512)
+            y = mm(self.context[...], tile(self.full[3], t * 512, 512)) + self.vec[BO : BO + 1, cols]
+            self.total[:, cols] = y + self.window[pl.ds(HALO, OWN), cols].astype(F32)
+            return carry
+
+        lax.fori_loop(0, 2, body, 0)
+
+    def norm_one(self):
+        def body(t, carry):
+            r = some_rows(t)
+            n, inv = normalized(self.total[r, :])
+            self.n1[r, :] = n
+            self.inv1[r, :] = jnp.broadcast_to(inv, (ROWS, 128))
+            y = n * self.vec[G1 : G1 + 1, :] + self.vec[S1 : S1 + 1, :]
+            self.normed[r, :] = y
+            self.low[r, :] = y.astype(BF)
+            return carry
+
+        lax.fori_loop(0, OWN // ROWS, body, 0)
+        self.both(self.low, self.low_out)
+        self.store(self.n1, self.n1_out)
+        self.store(self.inv1, self.inv1_out)
+
+    def feed_in(self, first, last):
+        feed_in(self.low, self.full[4], self.inner, self.act, self.slope, first, last)
+        if last == FF // 512:
+            self.both(self.act, self.act_out)
+            self.store(self.slope, self.slope_out)
+            self.store(self.vec, self.vec_out)
+
+    def feed_out(self):
+        self.store(self.full[5], self.weights_out[5])
+
+        def body(t, carry):
+            cols = columns(t * 512, 512)
+            y = mm(self.act[...], tile(self.full[5], t * 512, 512)) + self.vec[BU : BU + 1, cols]
+            self.total[:, cols] = y + self.normed[:, cols]
+            return carry
+
+        lax.fori_loop(0, 2, body, 0)
+
+    def cots_done(self):
+        self.view.cots_done()
+
+    def norm_two(self):
+        def body(t, carry):
+            r = some_rows(t)
+            n, inv = normalized(self.total[r, :])
+            gain = self.vec[G2 : G2 + 1, :]
+            self.encoded[r, :] = (n * gain + self.vec[S2 : S2 + 1, :]).astype(BF)
+            d = self.cots[r, :].astype(F32)
+            self.normed[r, :] = norm_back(d * gain, n, inv)
+            dn = jnp.sum((d * n).reshape(ROWS // 8, 8, D), axis=0)
+            return carry[0] + dn, carry[1] + jnp.sum(d.reshape(ROWS // 8, 8, D), axis=0)
+
+        zero = jnp.zeros((8, D), F32)
+        gain_sum, shift_sum = lax.fori_loop(0, OWN // ROWS, body, (zero, zero))
+        self.two[0:1, :] = jnp.sum(gain_sum, axis=0, keepdims=True)
+        self.two[1:2, :] = jnp.sum(shift_sum, axis=0, keepdims=True)
+        self.two[2:8, :] = jnp.zeros((6, D), F32)
+        self.store(self.normed, self.d_out)
+        self.store(self.encoded, self.encoded_out)
+        self.store(self.two, self.two_out)
+
+    def finish(self):
+        for got in self.gets:
+            got.wait_recv()
+        for move in self.stores:
+            move.wait()
+        self.net.finish()
+
+
+FORE = (
+    "begin", "a.p1", "b.p1", "u.p1", "vectors.along_z", "masks", "a.p2", "b.p2", "vectors.along_y", "a.p3",
+    "u.p2", "halo", "vectors.along_x", "a.p3_mid", "b.p3", "a.p3_core", "a.p3_end", "vectors.done", "u.p3",
+    "cots_in", "a.done", "query", "rows_done", "key", "b.p3_mid", "value", "keep_heads", "attend.0.2",
+    "b.p3_core", "attend.2.4", "b.p3_end", "u.p3_mid", "attend.4.6", "u.p3_core", "attend.6.8", "keep_probs",
+    "b.done", "mix", "norm_one", "feed_in.0.4", "u.p3_end", "feed_in.4.8", "u.done", "feed_out", "cots_done",
+    "norm_two", "finish",
+)
+
+
+def run_steps(work, steps):
+    for step in steps:
+        name, *rest = step.split(".")
+        if name in work.lanes:
+            each(work.lanes[name], rest[0])
+        elif name == "vectors":
+            getattr(work.vectors, rest[0])()
+        else:
+            getattr(work, name)(*map(int, rest))
+
+
 def forward_kernel(*refs):
-    tokens, cotangent, lengths, order, small = refs[:5]
-    own, refs = refs[5:11], refs[11:]
-    outs, refs = refs[:21], refs[21:]
-    weights_out, refs_out = outs[:6], outs[6:]
-    (x_out, q_out, k_out, v_out, probs_out, context_out, low_out, act_out, slope_out) = refs_out[:9]
-    (n1_out, inv1_out, d_final_out, encoded_out, vec_out, two_out) = refs_out[9:]
-    mine, peer = refs[:2]
-    full, refs = refs[2:8], refs[8:]
-    window, cots, q, k, v, probs, context, low, act, slope, bias, refs = *refs[:11], refs[11:]
-    n1, inv1, normed, total, encoded, vec, inner, two, refs = *refs[:8], refs[8:]
-    tiles, refs = refs[:5], refs[5:]
-    send_sem, recv_sem, local_sem = refs
-    net = Net(send_sem, recv_sem)
-    me, c = net.me, net.me["c"]
-    lo = lax.rem(me["y"], 2)
-    stores = []
-
-    def store(src, dst):
-        move = pltpu.make_async_copy(src, dst, local_sem.at[2 + len(stores)])
-        move.start()
-        stores.append(move)
-
-    def both(src, dst):
-        net.copy(src, dst.at[c], net.ring("c", 0))
-        store(src, dst.at[c])
-        return net.sent[-1]
-
-    for j in range(4):
-        mine[8 * j : 8 * j + 8, :] = own[j][...]
-        mine[32 + 8 * j : 40 + 8 * j, :] = own[4][:, 1024 * j : 1024 * j + 1024]
-    mine[64:96, :] = own[5][...]
-    net.barrier()
-    swap = net.copy(mine, peer, net.ring("c", 0))
-    vectors = Vectors(net, small, tiles, vec, inner)
-    vectors.start()
-    swap.wait_recv()
-    place_own(me, mine, peer, full)
-    rows = slice(None)
-    half = columns(c * 512, 512)
-    wi, wu = full[4], full[5]
-    first = [Gather(net, full[j], rows, half, ORDER[j]) for j in range(3)]
-    second = [
-        Gather(net, full[3], rows, half, ORDER[0]),
-        Gather(net, wi, rows, columns(c * 2048 + 512, 1024), ORDER[1]),
-        Gather(net, wi, rows, columns(c * 2048 + 1536, 512), ORDER[2]),
-        Gather(net, wi, rows, columns(c * 2048, 512), ORDER[0]),
-    ]
-    third = [
-        Gather(net, wu, pl.ds(0, 16), half, ORDER[0]),
-        Gather(net, wu, pl.ds(16, 16), half, ORDER[1]),
-        Gather(net, wu, pl.ds(32, 32), half, ORDER[2]),
-    ]
-    for lanes in (first, second, third):
-        each(lanes, "p1")
-    view = Window(net, tokens, cotangent, window, cots, local_sem)
-    view.start()
-    vectors.along_z()
-    segment_bias(lengths, order, me["x"] * OWN - HALO, lo, bias)
-    each(first, "p2")
-    vectors.along_y()
-    each(second, "p2")
-    each(third, "p2")
-    vectors.along_x()
-    each(first, "p3")
-    each(second, "p3")
-    each(first, "p3_mid")
-    each(third, "p3")
-    each(first, "p3_core")
-    vectors.done()
-    view.done()
-    each(second, "p3_mid")
-    each(first, "p3_end")
-    got_x = both(window, x_out)
-    each(first, "done")
-    project(window.at[pl.ds(HALO, OWN)], full[0], q, vec.at[BQ : BQ + 1])
-    each(third, "p3_mid")
-    project(window, full[1], k)
-    each(second, "p3_core")
-    project(window, full[2], v, vec.at[BV : BV + 1])
-    for j in range(3):
-        store(full[j], weights_out[j])
-    store(q, q_out)
-    store(k, k_out)
-    store(v, v_out)
-    attention(q, k, v, bias, probs, context, 0, 2)
-    each(second, "p3_end")
-    each(third, "p3_core")
-    attention(q, k, v, bias, probs, context, 2, 5)
-    each(third, "p3_end")
-    attention(q, k, v, bias, probs, context, 5, 8)
-    got_context = both(context, context_out)
-    store(probs, probs_out)
-    each(second, "done")
-    store(full[3], weights_out[3])
-    store(full[4], weights_out[4])
-
-    def attend(t, carry):
-        cols = columns(t * 512, 512)
-        y = mm(context[...], tile(full[3], t * 512, 512)) + vec[BO : BO + 1, cols]
-        total[:, cols] = y + window[pl.ds(HALO, OWN), cols].astype(F32)
-        return carry
-
-    lax.fori_loop(0, 2, attend, 0)
-
-    def norm_one(t, carry):
-        r = some_rows(t)
-        n, inv = normalized(total[r, :])
-        n1[r, :] = n
-        inv1[r, :] = jnp.broadcast_to(inv, (ROWS, 128))
-        y = n * vec[G1 : G1 + 1, :] + vec[S1 : S1 + 1, :]
-        normed[r, :] = y
-        low[r, :] = y.astype(BF)
-        return carry
-
-    lax.fori_loop(0, OWN // ROWS, norm_one, 0)
-    got_low = both(low, low_out)
-    store(n1, n1_out)
-    store(inv1, inv1_out)
-    feed_in(low, wi, inner, act, slope, 0, FF // 512)
-    got_act = both(act, act_out)
-    store(slope, slope_out)
-    store(vec, vec_out)
-    each(third, "done")
-    store(full[5], weights_out[5])
-
-    def feed_out(t, carry):
-        cols = columns(t * 512, 512)
-        y = mm(act[...], tile(wu, t * 512, 512)) + vec[BU : BU + 1, cols]
-        total[:, cols] = y + normed[:, cols]
-        return carry
-
-    lax.fori_loop(0, 2, feed_out, 0)
-
-    def norm_two(t, carry):
-        r = some_rows(t)
-        n, inv = normalized(total[r, :])
-        gain = vec[G2 : G2 + 1, :]
-        encoded[r, :] = (n * gain + vec[S2 : S2 + 1, :]).astype(BF)
-        d = cots[r, :].astype(F32)
-        normed[r, :] = norm_back(d * gain, n, inv)
-        dn = jnp.sum((d * n).reshape(ROWS // 8, 8, D), axis=0)
-        return carry[0] + dn, carry[1] + jnp.sum(d.reshape(ROWS // 8, 8, D), axis=0)
-
-    zero = jnp.zeros((8, D), F32)
-    gain_sum, shift_sum = lax.fori_loop(0, OWN // ROWS, norm_two, (zero, zero))
-    two[0:1, :] = jnp.sum(gain_sum, axis=0, keepdims=True)
-    two[1:2, :] = jnp.sum(shift_sum, axis=0, keepdims=True)
-    two[2:8, :] = jnp.zeros((6, D), F32)
-    store(normed, d_final_out)
-    store(encoded, encoded_out)
-    store(two, two_out)
-    for got in (got_x, got_context, got_low, got_act):
-        got.wait_recv()
-    for move in stores:
-        move.wait()
-    view.finish()
-    net.finish()
-
-
-def forward_all(tokens, cotangent, lengths, order, small, own):
+    run_steps(Forward(refs[:19], refs[19:40], refs[40:]), FORE)
+
+
+def forward_all(tokens, cotangent, lengths, order, own, small):
     any_space = pl.BlockSpec(memory_space=pl.ANY)
     vmem = pl.BlockSpec(memory_space=pltpu.VMEM)
     smem = pl.BlockSpec(memory_space=pltpu.SMEM)
@@ -643,13 +653,13 @@
     scratch += [((WIN, D), BF), ((OWN, D), BF), ((OWN, D), BF), ((WIN, D), BF), ((WIN, D), BF)]
     scratch += [((2, OWN, FF), BF), ((OWN, D), BF), ((OWN, D), BF), ((OWN, FF), BF), ((OWN, FF), BF)]
     scratch += [((2, SPAN, TOK), F32), ((OWN, D), F32), ((OWN, 128), F32), ((OWN, D), F32), ((OWN, D), F32)]
-    scratch += [((OWN, D), BF), ((8, D), F32), ((1, FF), F32), ((8, D), F32)]
+    scratch += [((OWN, D), BF), ((8, D), F32), ((1, FF), F32), ((8, D), F32), ((16, 128), F32)]
     scratch += [((16, 128), BF)] * 2 + [((4, 16, 128), BF)] * 2 + [((4, 2, 16, 128), BF)]
     return pl.pallas_call(
         forward_kernel,
         name="forward_all",
         out_shape=[jax.ShapeDtypeStruct(s, t) for s, t in full + kept],
-        in_specs=[any_space] * 2 + [smem] * 2 + [vmem] * 7,
+        in_specs=[any_space] * 2 + [smem] * 2 + [vmem] * 15,
         out_specs=[any_space] * 21,
         scratch_shapes=[pltpu.VMEM(s, t) for s, t in scratch]
         + [
@@ -658,7 +668,7 @@
             pltpu.SemaphoreType.DMA((32,)),
         ],
         compiler_params=pltpu.CompilerParams(collective_id=1, has_side_effects=True, vmem_limit_bytes=62 << 20),
-    )(tokens, cotangent, lengths, order, small, *own)
+    )(tokens, cotangent, lengths, order, *own, *small)
 
 
 def add_into(dst, srcs):
@@ -750,9 +760,9 @@
     (5, (16, 16), (0, 512), 1),
     (5, (32, 32), (0, 512), 2),
     (4, (0, 16), (0, 512), 0),
-    (4, (0, 16), (512, 1024), 1),
-    (4, (0, 16), (1536, 512), 2),
-    (3, (0, 16), (0, 512), 0),
+    (4, (0, 16), (512, 512), 1),
+    (4, (0, 16), (1024, 1024), 2),
+    (3, (0, 16), (0, 512), 1),
     (0, (0, 16), (0, 512), 0),
     (1, (0, 16), (0, 512), 1),
     (2, (0, 16), (0, 512), 2),
@@ -830,8 +840,9 @@
         out[...] = jnp.broadcast_to(jnp.sum(jnp.where(keep, got, 0.0), axis=0, keepdims=True), (8, 128))
 
 
-def attention_back(q, k, v, probs, context, d_context, dq, dk, dv, first, last):
-    def body(h, carry):
+def attention_back(q, k, v, probs, context, d_context, dq, dk, dv, first, last, start):
+    def body(i, carry):
+        h = lax.rem(i + start, HEADS // 2)
         cols = columns(h * 128, 128)
         dks, dvs = [], []
         for b in range(2):
@@ -864,77 +875,44 @@
 
 
 class Return:
-    def __init__(self, net, window, encoded, back, out, local_sem):
-        self.net = net
-        lo = lax.rem(net.me["y"], 2)
-        other = 1 - lo
-        self.lo = lo
-        self.window, self.back = window, back
-        self.plain = [(window.at[rows_at(HALO + TOK * other, TOK)], back.at[0, lo], net.pair(0, other))]
-        self.encoded = (encoded.at[rows_at(TOK * other, TOK)], out.at[lo], net.pair(0, other))
-        self.local = pltpu.make_async_copy(encoded.at[rows_at(TOK * lo, TOK)], out.at[lo], local_sem)
-        self.base = net.used
-        net.used += 16
+    def __init__(self, net, window, encoded, back, out, token_grad, sems):
+        self.net, self.window, self.encoded, self.back = net, window, encoded, back
+        self.out, self.token_grad, self.sems = out, token_grad, sems
+        self.swaps = []
+        self.lo = lax.rem(net.me["y"], 2)
+
+    def pair(self, src, dst, sem):
+        mine, theirs = rows_at(TOK * self.lo, TOK), rows_at(TOK * (1 - self.lo), TOK)
+        local = pltpu.make_async_copy(src.at[mine], dst.at[self.lo], sem)
+        local.start()
+        return local, self.net.copy(src.at[theirs], dst.at[self.lo], self.net.pair(1 - self.lo))
 
     def start_encoded(self):
-        self.encoded = self.net.copy(*self.encoded)
-        self.local.start()
+        self.swaps.append(self.pair(self.encoded, self.out, self.sems.at[0]))
 
     def start(self):
-        net, lo = self.net, self.lo
-        self.plain = [net.copy(*p) for p in self.plain] + [self.encoded]
-        self.copies = []
-        for k in range(4):
-            for q in range(2):
-                by, rows, to, only = pieces(q)[k]
-                if only is not None and only != q:
-                    continue
-                side = 1 if by == 1 else 2
-                copy = net.make(
-                    self.window.at[pl.ds(to, TOK // 2)],
-                    self.back.at[side, lo, rows],
-                    net.pair(-by, q),
-                    self.base + 4 * k + q,
-                    self.base + 4 * k + 2 + lo,
-                )
-                copy.start()
-                self.copies.append(copy)
-
-    def gets(self):
-        net = self.net
-        for copy in self.plain:
-            copy.wait_recv()
-        for k in range(4):
-            _, rows, _, only = pieces(0)[k]
-            for m in range(2):
-                copy = net.make(
-                    self.window.at[pl.ds(0, TOK // 2)],
-                    self.back.at[1, m, rows],
-                    net.pair(1, 0),
-                    0,
-                    self.base + 4 * k + 2 + m,
-                )
-                if only is None:
-                    copy.wait_recv()
-                else:
-                    pl.when(self.lo == only)(copy.wait_recv)
-
-    def total(self, token_grad):
-        lo = self.lo
-        half = TOK // 2
-        own = self.window[rows_at(HALO + TOK * lo, TOK), :].astype(F32)
-        for m in range(2):
-            base = jnp.where(lo == m, own, self.back[0, m].astype(F32))
-            right = self.back[1, m].astype(F32)
-            left = self.back[2, m].astype(F32)
-            low = base[:half] + left[:half] + jnp.where(lo == 1, right[:half], 0.0)
-            high = base[half:] + right[half:] + jnp.where(lo == 0, left[half:], 0.0)
-            token_grad[m] = jnp.concatenate([low, high], axis=0).astype(BF)
-
-    def finish(self):
-        self.local.wait()
-        for copy in self.copies:
-            copy.wait_send()
+        w, net = self.window, self.net
+        self.c = [
+            net.copy(w.at[pl.ds(0, HALO)], self.back.at[0], net.ring("x", 3)),
+            net.copy(w.at[pl.ds(HALO + OWN, HALO)], self.back.at[1], net.ring("x", 1)),
+        ]
+
+    def total(self):
+        for moved in self.c:
+            moved.wait_recv()
+        rest = OWN - HALO
+        own = pl.ds(HALO, OWN)
+        y = self.window[own, :].astype(F32)
+        low = y[:rest] + self.back[1, :rest].astype(F32)
+        mid = y[rest:HALO] + self.back[1, rest:].astype(F32) + self.back[0, : HALO - rest].astype(F32)
+        high = y[HALO:] + self.back[0, HALO - rest :].astype(F32)
+        self.window[own, :] = jnp.concatenate([low, mid, high], axis=0).astype(BF)
+        self.swaps.append(self.pair(self.window.at[own], self.token_grad, self.sems.at[1]))
+
+    def done(self):
+        for local, moved in self.swaps:
+            local.wait()
+            moved.wait_recv()
 
 
 class Stream:
@@ -984,6 +962,7 @@
         self.x, self.q, self.k, self.v, self.context, self.low, self.act, self.inner, self.n1, self.inv1, self.d = nxt(11)
         self.outer, self.outer_sib, self.inner_sib, self.branch, self.branch_sib, self.d_context = nxt(6)
         self.dq, self.dk, self.dv, self.dq_sib, self.dk_sib, self.dv_sib, self.dx, self.back = nxt(8)
+        self.kept, self.low_t = nxt(2)
         self.total, *vector_bufs = nxt(8)
         self.finals, self.ends = nxt(6), nxt(6)
         send_sem, recv_sem, self.local_sem = nxt(3)
@@ -992,7 +971,9 @@
         self.loads = 0
         self.stream = Stream(self.weights, self.ring, self.local_sem.at[pl.ds(0, 48)])
         self.vectors = VectorSum(self.net, self.total, vector_bufs)
-        self.back_rows = Return(self.net, self.dx, self.encoded, self.back, self.out, self.local_sem.at[48])
+        self.back_rows = Return(
+            self.net, self.dx, self.kept, self.back, self.out, self.token_grad, self.local_sem.at[pl.ds(48, 2)]
+        )
         lanes = []
         for n, (w, (r0, rows), (base, width), order) in enumerate(RECTS):
             lanes.append(
@@ -1008,7 +989,7 @@
         self.lanes = {"u": lanes[:3], "i": lanes[3:6], "o": lanes[6:7], "a": lanes[7:]}
 
     def load(self, src, dst):
-        move = pltpu.make_async_copy(src, dst, self.local_sem.at[49 + self.loads])
+        move = pltpu.make_async_copy(src, dst, self.local_sem.at[50 + self.loads])
         self.loads += 1
         move.start()
         return move
@@ -1020,13 +1001,30 @@
         return self.net.copy(src.at[:, self.half(1 - self.c, width)], dst, self.net.ring("c", 0))
 
     def begin(self):
-        self.at_d = self.load(self.d_in, self.d)
-        for n in range(4):
+        greeted = self.net.greet()
+        at_d = self.load(self.d_in, self.d)
+        self.stream.start(0)
+        self.total[...] = jnp.zeros((16, D), F32)
+        self.total[G2 : G2 + 2, :] = self.two[0:2, :]
+        at_d.wait()
+        self.at_slope = self.load(self.slope_in, self.inner)
+        for n in range(1, 4):
             self.stream.start(n)
-        self.at_slope = self.load(self.slope_in, self.inner)
+
+        def body(t, carry):
+            r = some_rows(t)
+            low = self.d[r, :].astype(BF)
+            self.outer[r, :] = low
+            return carry + jnp.sum(low.astype(F32).reshape(ROWS // 8, 8, D), axis=0)
+
+        s = lax.fori_loop(0, OWN // ROWS, body, jnp.zeros((8, D), F32))
+        self.total[BU : BU + 1, :] = jnp.sum(s, axis=0, keepdims=True)
+        greeted()
+        self.got_outer = self.share(self.outer, self.outer_sib, 512)
         self.at_act = self.load(self.act_in, self.act)
         self.at_low = self.load(self.low_in, self.low)
         self.at_n1 = [self.load(self.n1_in, self.n1), self.load(self.inv1_in, self.inv1)]
+        self.at_kept = self.load(self.encoded, self.kept)
         self.at_rest = [
             self.load(self.context_in, self.context),
             self.load(self.x_in, self.x),
@@ -1034,21 +1032,6 @@
             self.load(self.k_in, self.k),
             self.load(self.v_in, self.v),
         ]
-        self.total[...] = jnp.zeros((16, D), F32)
-        self.total[G2 : G2 + 2, :] = self.two[0:2, :]
-        self.at_d.wait()
-
-        def body(t, carry):
-            r = some_rows(t)
-            low = self.d[r, :].astype(BF)
-            self.outer[r, :] = low
-            return carry + jnp.sum(low.astype(F32).reshape(ROWS // 8, 8, D), axis=0)
-
-        s = lax.fori_loop(0, OWN // ROWS, body, jnp.zeros((8, D), F32))
-        self.total[BU : BU + 1, :] = jnp.sum(s, axis=0, keepdims=True)
-        self.net.barrier()
-        self.got_outer = self.share(self.outer, self.outer_sib, 512)
-        self.back_rows.start_encoded()
 
     def d_inner(self):
         self.at_slope.wait()
@@ -1096,16 +1079,22 @@
             self.d[:, cols] = y
             self.stream.start(8 + n)
 
+    def turn_low(self):
+        self.at_low.wait()
+        for j, which in enumerate((self.c, 1 - self.c)):
+            for x in range(4):
+                part = self.low[which, :, 256 * x : 256 * x + 256]
+                self.low_t[256 * x : 256 * x + 256, OWN * j : OWN * j + OWN] = part.T
+
     def grad_inner(self):
-        self.at_low.wait()
         self.got_inner.wait_recv()
         c = self.c
 
         def body(t, carry):
             x, j = lax.div(t, 4), lax.rem(t, 4)
-            rows, cols = columns(x * 256, 256), columns(j * 512, 512)
-            y = mm(self.low[c, :, rows], self.inner[:, columns(c * 2048 + j * 512, 512)], TN)
-            y = y + mm(self.low[1 - c, :, rows], self.inner_sib[:, cols], TN)
+            rows, cols = pl.ds(pl.multiple_of(x * 256, 256), 256), columns(j * 512, 512)
+            y = mm(self.low_t[rows, :OWN], self.inner[:, columns(c * 2048 + j * 512, 512)])
+            y = y + mm(self.low_t[rows, OWN:], self.inner_sib[:, cols])
             self.g[4][x, :, :, :, :, cols] = y.astype(BF).reshape(2, 2, 4, 16, 512)
             return carry
 
@@ -1171,6 +1160,7 @@
             self.dv,
             first,
             last,
+            HEADS // 4 * (1 - self.c),
         )
 
     def share_heads(self):
@@ -1179,6 +1169,8 @@
             self.share(self.dv, self.dv_sib, 512),
             self.share(self.dq, self.dq_sib, 512),
         ]
+
+    def head_sums(self):
         self.total[BQ : BQ + 1, :] = column_sum(self.dq[...])
         self.total[BV : BV + 1, :] = column_sum(self.dv[...])
         self.vectors.start()
@@ -1197,17 +1189,35 @@
         rows = (self.x.at[self.c, own], self.x.at[1 - self.c, own])
         self.grad_rows(rows, self.dq, self.dq_sib, self.g[0])
 
-    def d_tokens(self):
-        for n in (9, 10, 11):
+    def d_halo(self):
+        for n in (9, 10):
             self.stream.wait(n)
+
+        def sides(ref):
+            return jnp.concatenate([ref[:HALO, :], ref[HALO + OWN :, :]], axis=0)
+
         for x in range(4):
             cols = slice(256 * x, 256 * x + 256)
-            y = mm(self.dk[...], self.stream.part(9, x), NT) + mm(self.dv[...], self.stream.part(10, x), NT)
-            own = self.d[:, cols] + mm(self.dq[...], self.stream.part(11, x), NT)
+            y = mm(sides(self.dk), self.stream.part(9, x), NT) + mm(sides(self.dv), self.stream.part(10, x), NT)
             self.dx[:HALO, cols] = y[:HALO].astype(BF)
-            self.dx[HALO : HALO + OWN, cols] = (y[HALO : HALO + OWN] + own).astype(BF)
-            self.dx[HALO + OWN :, cols] = y[HALO + OWN :].astype(BF)
+            self.dx[HALO + OWN :, cols] = y[HALO:].astype(BF)
         self.back_rows.start()
+
+    def d_own(self):
+        self.stream.wait(11)
+        own = slice(HALO, HALO + OWN)
+        for x in range(4):
+            cols = slice(256 * x, 256 * x + 256)
+            y = mm(self.dk[own, :], self.stream.part(9, x), NT) + mm(self.dv[own, :], self.stream.part(10, x), NT)
+            y = y + self.d[:, cols] + mm(self.dq[...], self.stream.part(11, x), NT)
+            self.dx[own, cols] = y.astype(BF)
+
+    def encoded_out(self):
+        self.at_kept.wait()
+        self.back_rows.start_encoded()
+
+    def rows_back(self):
+        self.back_rows.total()
 
     def finish(self):
         c, net = self.c, self.net
@@ -1224,8 +1234,6 @@
             given = final.at[pl.ds(pl.multiple_of(n * (1 - c), 8), n)]
             swaps.append((w, net.copy(given, end.at[:, columns(c * width, width)], net.ring("c", 0))))
             end[:, columns(c * width, width)] = kept[...]
-        self.back_rows.gets()
-        self.back_rows.total(self.token_grad)
         self.vectors.done(self.small)
         stores = []
         for w, swap in swaps:
@@ -1233,28 +1241,17 @@
             stores.append(self.load(self.ends[w], self.owned[w]))
         for store in stores:
             store.wait()
-        self.back_rows.finish()
+        self.back_rows.done()
         net.finish()
 
 
 BACK = (
-    "begin", "d_inner", "grad_outer", "u.p1", "d_normed", "u.p1_mid", "grad_inner", "i.p1", "norm_one",
-    "d_mixed", "u.p2", "i.p1_mid", "grad_output", "o.p1", "attend.0.3", "u.p3", "i.p2", "attend.3.6",
-    "o.p1_mid", "i.p3", "attend.6.8", "share_heads", "d_tokens", "grad_key", "grad_value", "grad_query",
-    "a.p1", "vectors.along_x", "o.p2", "vectors.along_y", "a.p1_mid", "o.p3", "vectors.along_z", "a.p2",
-    "a.p3", "finish",
+    "begin", "grad_outer", "u.p1", "encoded_out", "d_inner", "d_normed", "u.p1_mid", "norm_one", "turn_low",
+    "d_mixed", "grad_output", "o.p1", "grad_inner", "i.p1", "attend.0.4", "share_heads", "u.p2", "attend.4.8",
+    "o.p1_mid", "i.p1_mid", "head_sums", "d_halo", "grad_key", "grad_value", "grad_query", "a.p1", "d_own",
+    "u.p3", "vectors.along_x", "i.p2", "a.p1_mid", "vectors.along_y", "o.p2", "rows_back", "i.p3",
+    "vectors.along_z", "a.p2", "o.p3", "a.p3", "finish",
 )
-
-
-def run_steps(work, steps):
-    for step in steps:
-        name, *rest = step.split(".")
-        if name in work.lanes:
-            each(work.lanes[name], rest[0])
-        elif name == "vectors":
-            getattr(work.vectors, rest[0])()
-        else:
-            getattr(work, name)(*map(int, rest))
 
 
 def backward_kernel(*refs):
@@ -1272,7 +1269,7 @@
     scratch += [((2, OWN, FF), BF), ((OWN, FF), BF), ((OWN, D), F32), ((OWN, 128), F32), ((OWN, D), F32)]
     scratch += [((OWN, D), BF), ((OWN, 512), BF), ((OWN, 2048), BF), ((OWN, D), BF), ((OWN, 512), BF), ((OWN, D), BF)]
     scratch += [((OWN, D), BF), ((WIN, D), BF), ((WIN, D), BF), ((OWN, 512), BF), ((WIN, 512), BF), ((WIN, 512), BF)]
-    scratch += [((WIN, D), BF), ((3, 2, TOK, D), BF)]
+    scratch += [((WIN, D), BF), ((2, HALO, D), BF), ((OWN, D), BF), ((D, 2 * OWN), BF)]
     scratch += [((16, D), F32), ((16, D), F32), ((16, D), F32), ((3, 16, 256), F32), ((2, 16, 128), F32), ((3, 16, 128), F32)]
     scratch += [((16, 128), F32), ((3, 16, 128), F32)]
     scratch += [((r, n // 2), F32) for r, n in BLOCKS] + [(s, F32) for s in owned]
@@ -1283,7 +1280,7 @@
         + [jax.ShapeDtypeStruct((2, TOK, D), BF)] * 2
         + [jax.ShapeDtypeStruct((8, 128), F32)],
         in_specs=[any_space] * 19 + [vmem] * 2,
-        out_specs=[any_space] * 7 + [vmem] * 2,
+        out_specs=[any_space] * 8 + [vmem],
         scratch_shapes=[pltpu.VMEM(s, t) for s, t in scratch]
         + [
             pltpu.SemaphoreType.DMA((N_SEM,)),
@@ -1294,14 +1291,30 @@
     )(*kept)
 
 
+def keep_kernel(*refs):
+    for src, dst in zip(refs[:8], refs[8:]):
+        dst[...] = src[...]
+
+
+def keep(*arrays):
+    return pl.pallas_call(
+        keep_kernel,
+        name="keep",
+        out_shape=[jax.ShapeDtypeStruct(a.shape, a.dtype) for a in arrays],
+        in_specs=[pl.BlockSpec(memory_space=pltpu.VMEM)] * 8,
+        out_specs=[pl.BlockSpec(memory_space=pltpu.VMEM)] * 8,
+    )(*arrays)
+
+
 def local(
     tokens, cotangent, seq_lengths, block_offsets, deal_order, wq, wk, wv, wo, bq, bv, bo, g1, s1, wi, bi, wu, bu, g2, s2
 ):
-    small = jnp.pad(jnp.concatenate([bq, bv, bo, g1, s1, bu, g2, s2, bi]), (0, 32))[None]
+    small = [v[None] for v in (bq, bv, bo, g1, s1, bu, g2, s2, bi)]
     kept = forward_all(
-        tokens[:, 0], cotangent[:, 0], seq_lengths[:, 0], deal_order[:, 0], small, (wq, wk, wv, wo, wi, wu)
+        tokens[:, 0], cotangent[:, 0], seq_lengths[:, 0], deal_order[:, 0], (wq, wk, wv, wo, wi, wu), small
     )
     *owned, out, token_grad, sums = backward_all(kept)
+    *owned, out, token_grad = keep(*owned, out, token_grad)
     mine = sums[0]
     sbq, sbv, sbo, sg1, ss1, sbu, sg2, ss2 = [mine[8 * j : 8 * j + 8] for j in range(8)]
     return (

time: 226 us -> 184 us (0.81)
  Pallas kernels: 207 us -> 180 us
  local copies, waits for them, and re-layouts: 17 us -> 2.81 us
    pallas_call x1, Pallas kernels: 107 us -> 86.4 us  [backward_all(): pl.pallas_call(backward_kernel, name='backward_all', out_shape=[jax.Shape...]
    pallas_call x1, Pallas kernels: 100 us -> 90.6 us  [forward_all(): pl.pallas_call(forward_kernel, name='forward_all', out_shape=[jax.ShapeDt...]
    unnamed x20 -> x0, local copies, waits for them, and re-layouts: 7.53 us -> none
    concatenate x1 -> x0, local copies, waits for them, and re-layouts: 6.1 us -> none  [local(): jnp.concatenate([bq, bv, bo, g1, s1, bu, g2, s2, bi])]
    pallas_call x0 -> x1, Pallas kernels: none -> 2.51 us  [keep(): pl.pallas_call(keep_kernel, name='keep', out_shape=[jax.ShapeDtypeStruct(...]
where the time goes in v3:
time: 184 us; the launch traced here: 183 us
  Pallas kernels  180 us (98%)
  local copies, waits for them, and re-layouts  2.81 us (2%)
    pallas_call x1, Pallas kernels, forward_all(): pl.pallas_call(forward_kernel, name='forward_all', out_shape=[jax.ShapeDt...  90.6 us
    pallas_call x1, Pallas kernels, backward_all(): pl.pallas_call(backward_kernel, name='backward_all', out_shape=[jax.Shape...  86.4 us

profile of v3, /device:TPU:1, one launch (start us, length us, event | category | flops | bytes accessed | tf_op | source)
XLA Modules:
  0.0 183.2 jit_solution(13604391175145024601)
XLA Ops:
  0.7 90.6 %forward_all.1 = (bf16[4,2,2,4,16,1024]{5,4,3,2,1,0:T(8,128)(2,1)}, bf16[4,2,2,4,16,1024]{5,4,3,2,1,0:T(8,128)(2,1)}, bf16[4,2,2,4,16,1024]{5,4,3,2,1,0:T(8,128)...) custom-call(bf16[2,128,1024]{2,1,0:T(8,128)(2,1)} %bitcast.37, ...), custom_call_target="tpu_custom_call" | custom-call | tf_op jit(solution)/shard_map/forward_all/pallas_call | solution.py:658
  91.3 86.4 %backward_all.1 = (f32[8,1024]{1,0:T(8,128)}, f32[8,1024]{1,0:T(8,128)}, f32[8,1024]{1,0:T(8,128)}, f32[8,1024]{1,0:T(8,128)}, f32[8,4096]{1,0:T(8,128)}, /*inde...) custom-call(bf16[4,2,2,4,16,1024]{5,4,3,2,1,0:T(8,128)(2,1)} %get-tuple-element., ...), custom_call_target="tpu_custom_call" | custom-call | tf_op jit(solution)/shard_map/backward_all/pallas_call | solution.py:1276
  177.8 2.5 %keep.1 = (f32[8,1024]{1,0:T(8,128)}, f32[8,1024]{1,0:T(8,128)}, f32[8,1024]{1,0:T(8,128)}, f32[8,1024]{1,0:T(8,128)}, f32[8,4096]{1,0:T(8,128)}, /*index=5*/f32...) custom-call(f32[8,1024]{1,0:T(8,128)} %get-tuple-element.76.refs_0_, ...), custom_call_target="tpu_custom_call" | custom-call | tf_op jit(solution)/shard_map/keep/pallas_call | solution.py:1300
  180.3 1.2 slice_bitcast_fusion.3
  181.5 1.6 slice_bitcast_fusion
